TPU v7x, 128 devices: a whole 4x4x4 slice. The times are simulated.
128 devices in a mesh: index: 16 (over y, x_hi, core), rep: 4 (over z), tp: 2 (over x_lo).
Axes of the slice: x: 4 (x_hi: 2, x_lo: 2; x = x_hi * 2 + x_lo), y: 4, z: 4, core: 2. Of those that a mesh axis runs over, the one named last changes fastest.
Arguments:
- queries: bfloat16 [2048, 1024], P(('index', 'rep', 'tp')), may hold values from -150 to 150
- passages: bfloat16 [32768, 1024], P('index'), may hold values from -30 to 30
- probe_owner: int32 [2048, 4], P(('index', 'rep', 'tp')), may hold values from 0 to 15, all different within a row; in each aligned block of 16 rows (0 to 15, 16 to 31, ...) at most 8 rows name the same one
- probe_cluster: int32 [2048, 4], P(('index', 'rep', 'tp')), may hold values from 0 to 3
- pair_owner: int32 [2048, 64, 1], P(('index', 'rep', 'tp')), may hold values from 0 to 15; in each aligned block of 1024 rows (0 to 1023, 1024 to 2047, ..., all dimensions but the last counted through in order) at most 128 rows name the same one
- pair_row: int32 [2048, 64], P(('index', 'rep', 'tp')), may hold values from 0 to 2047
- w_qkv: bfloat16 [1024, 3, 1024], P(None, None, 'tp'), may hold values from -0.046875 to 0.046875
- w_out: bfloat16 [1024, 1024], P('tp'), may hold values from -0.375 to 0.375
- w_up: bfloat16 [1024, 4096], P(None, 'tp'), may hold values from -0.1875 to 0.1875
- w_down: bfloat16 [4096, 1024], P('tp'), may hold values from -0.09375 to 0.09375
- gain_one: float32 [1024], replicated, may hold values from 0.1 to 1.9
- gain_two: float32 [1024], replicated, may hold values from 0.1 to 1.9
Outputs:
- reranked: bfloat16 [2048, 65, 1024], P(('index', 'rep', 'tp'))
Inputs may be any that keep to these rules, and one draw needn't show every extreme that they name: `probe_owner`: each query names 4 different owners; within the queries of one device (aligned blocks of 16 queries) no owner is named more than 8 times, a bound that some block reaches. `pair_owner`: within the candidates of one device (aligned blocks of 1024) no owner is named more than 128 times, a bound that some block reaches.
All inputs are finite; a program needn't handle non-finite values.
Results may differ from a plain program's by a relative error of at most 0.013.
Values may be sent and summed in bfloat16 or wider, within the bound.
A program may use at most 192 MiB of HBM per device.

v0:
```python
import jax
import jax.numpy as jnp
from jax import lax
from jax.sharding import PartitionSpec as P

D = 1024
HD = 64
K = 64
NPROBE = 4
CL_DEV = 4
CL_ROWS = 512
Q_DEV = 16
S = 65
PASS_DEV = 2048


def layer_norm(values, scale_gain):
    center_mean = jnp.mean(values, -1, keepdims=True)
    centered = values - center_mean
    variance = jnp.mean(centered * centered, -1, keepdims=True)
    return centered * lax.rsqrt(variance + 1e-05) * scale_gain


def slot_numbers(owner_ids, owner_count):
    onehot = (owner_ids[:, None] == jnp.arange(owner_count, dtype=jnp.int32)[None, :]).astype(
        jnp.int32
    )
    before = jnp.cumsum(onehot, 0) - onehot
    return jnp.sum(before * onehot, 1)


def attend(qkv, head_count):
    lists = qkv.shape[0]
    shaped = qkv.reshape(lists, S, 3, head_count, HD)
    scores = jnp.einsum(
        "gshe,gthe->ghst", shaped[:, :, 0], shaped[:, :, 1], preferred_element_type=jnp.float32
    ) * HD ** (-0.5)
    probs = jax.nn.softmax(scores, -1).astype(jnp.bfloat16)
    context = jnp.einsum(
        "ghst,gthe->gshe", probs, shaped[:, :, 2], preferred_element_type=jnp.float32
    )
    return context.astype(jnp.bfloat16).reshape(lists, S, head_count * HD)


def on_device(
    queries,
    passages,
    probe_owner,
    probe_cluster,
    pair_owner,
    pair_row,
    w_qkv,
    w_out,
    w_up,
    w_down,
    gain_one,
    gain_two,
):
    f32 = jnp.float32
    bf16 = jnp.bfloat16
    owner_count = lax.axis_size("index")
    probe_cap = max(2, min(Q_DEV, (2 * Q_DEV * NPROBE + owner_count - 1) // owner_count))
    pair_cap = max(2, min(Q_DEV * K, (2 * Q_DEV * K + owner_count - 1) // owner_count))
    probe_flat = probe_owner.reshape(-1)
    probe_slot = slot_numbers(probe_flat, owner_count)
    probe_dest = probe_flat * probe_cap + probe_slot
    query_rows = jnp.broadcast_to(queries[:, None, :], (Q_DEV, NPROBE, D)).reshape(-1, D)
    cluster_marks = (
        probe_cluster.reshape(-1)[:, None] == jnp.arange(CL_DEV, dtype=jnp.int32)[None, :]
    ).astype(bf16)
    send_rows = jnp.zeros((owner_count * probe_cap, D), bf16).at[probe_dest].set(query_rows)
    send_marks = (
        jnp.zeros((owner_count * probe_cap, CL_DEV), bf16).at[probe_dest].set(cluster_marks)
    )
    pair_flat = pair_owner.reshape(-1)
    pair_slot = slot_numbers(pair_flat, owner_count)
    pair_dest = pair_flat * pair_cap + pair_slot
    row_flat = pair_row.reshape(-1)
    digits = jnp.stack([row_flat // 32, row_flat % 32], 1).astype(bf16)
    send_digits = jnp.zeros((owner_count * pair_cap, 2), bf16).at[pair_dest].set(digits)
    got_rows, got_marks, got_digits = (
        lax.all_to_all(
            send_rows.reshape(owner_count, probe_cap, D),
            "index",
            split_axis=0,
            concat_axis=0,
            tiled=True,
        ),
        lax.all_to_all(
            send_marks.reshape(owner_count, probe_cap, CL_DEV),
            "index",
            split_axis=0,
            concat_axis=0,
            tiled=True,
        ),
        lax.all_to_all(
            send_digits.reshape(owner_count, pair_cap, 2),
            "index",
            split_axis=0,
            concat_axis=0,
            tiled=True,
        ),
    )
    flat_rows = got_rows.reshape(-1, D)
    flat_marks = got_marks.reshape(-1, CL_DEV)
    membership = (
        jnp.arange(PASS_DEV, dtype=jnp.int32)[None, :] // CL_ROWS
        == jnp.arange(CL_DEV, dtype=jnp.int32)[:, None]
    ).astype(bf16)
    allowed = jnp.dot(flat_marks, membership, preferred_element_type=f32)
    scores = jnp.einsum("md,pd->mp", flat_rows, passages, preferred_element_type=f32) * D ** (-0.5)
    masked = jnp.where(allowed > 0.5, scores, -1e30)
    peak = jnp.max(masked, 1, keepdims=True)
    expo = jnp.exp(masked - peak) * allowed
    denom = jnp.sum(expo, 1, keepdims=True) + (1.0 - jnp.max(allowed, 1, keepdims=True))
    weights = (expo / denom).astype(bf16)
    pooled = jnp.dot(weights, passages, preferred_element_type=f32).astype(bf16)
    fetch_ids = (
        (got_digits[..., 0].astype(f32) * 32.0 + got_digits[..., 1].astype(f32))
        .astype(jnp.int32)
        .reshape(-1)
    )
    fetched = jnp.take(passages, fetch_ids, axis=0)
    reply = jnp.concatenate(
        [pooled.reshape(owner_count, probe_cap, D), fetched.reshape(owner_count, pair_cap, D)], 1
    )
    returned = lax.all_to_all(reply, "index", split_axis=0, concat_axis=0, tiled=True).reshape(
        -1, D
    )
    slot_width = probe_cap + pair_cap
    answers = jnp.take(returned, probe_flat * slot_width + probe_slot, axis=0).astype(f32)
    retrieval = jnp.sum(answers.reshape(Q_DEV, NPROBE, D), 1) / NPROBE
    lead = (queries.astype(f32) + retrieval).astype(bf16)
    candidates = jnp.take(returned, pair_flat * slot_width + probe_cap + pair_slot, axis=0).reshape(
        Q_DEV, K, D
    )
    tokens = jnp.concatenate([lead[:, None, :], candidates], 1)
    head_count = w_qkv.shape[2] // HD
    all_tokens = lax.all_gather(tokens, "tp", axis=0, tiled=True)
    qkv = jnp.einsum("gsd,dcf->gscf", all_tokens, w_qkv, preferred_element_type=f32).astype(bf16)
    context = attend(qkv, head_count)
    partial_attn = jnp.einsum("gsf,fd->gsd", context, w_out, preferred_element_type=f32)
    attn = lax.psum(partial_attn.astype(jnp.bfloat16), "tp").astype(jnp.float32)
    hidden_all = layer_norm(all_tokens.astype(f32) + attn, gain_one).astype(bf16)
    active = jax.nn.gelu(
        jnp.einsum("gsd,df->gsf", hidden_all, w_up, preferred_element_type=f32), approximate=False
    ).astype(bf16)
    hidden_own = lax.dynamic_slice_in_dim(hidden_all, lax.axis_index("tp") * Q_DEV, Q_DEV, 0)
    down = lax.psum_scatter(
        jnp.einsum("gsf,fd->gsd", active, w_down, preferred_element_type=f32).astype(jnp.bfloat16),
        "tp",
        scatter_dimension=0,
        tiled=True,
    ).astype(jnp.float32)
    return layer_norm(hidden_own.astype(f32) + down, gain_two).astype(bf16)


def solution(mesh):
    in_specs = (
        P(("index", "rep", "tp"), None),
        P("index", None),
        P(("index", "rep", "tp"), None),
        P(("index", "rep", "tp"), None),
        P(("index", "rep", "tp"), None, None),
        P(("index", "rep", "tp"), None),
        P(None, None, "tp"),
        P("tp", None),
        P(None, "tp"),
        P("tp", None),
        P(),
        P(),
    )
    out_specs = P(("index", "rep", "tp"), None, None)
    return jax.shard_map(
        on_device, mesh=mesh, in_specs=in_specs, out_specs=out_specs, check_vma=False
    )
```

profile of v0, /device:TPU:1, one launch (start us, length us, event | category | flops | bytes accessed | tf_op | source)
XLA Modules:
  0.0 568.7 jit_solution(7302043870958473391)
XLA Ops:
  6.5 0.9 copy.105
  7.4 0.1 reshape.452
  7.5 0.7 broadcast_multiply_fusion.3
  8.3 0.1 reduce_window_sum.26
  8.4 0.2 select_reduce_fusion
  8.6 0.1 mul.180
  8.7 0.1 copy.107
  8.8 0.1 mul.170
  8.9 0.8 copy.108
  9.6 0.1 eq.71
  9.7 0.8 scatter_custom_fusion
  10.6 0.8 copy.110
  11.3 8.4 %all-to-all-start = ((bf16[16,8,4]{1,2,0:T(4,128)(2,1)}), bf16[16,8,4]{1,2,0:T(4,128)(2,1)S(1)}, u32[]{:S(2)}, u32[]{:S(2)}) async-start(bf16[16,8,4]{1,2,0:T(4,128)(2,1)} %copy.110), calls=%async_computation | async-start | bytes 32768 | tf_op jit(solution)/shard_map/all_to_all | solution.py:89
  19.8 0.5 broadcast.445
  20.3 1.4 fusion.95
  21.8 0.8 eq.82
  22.6 4.5 reduce-window.6
  27.1 0.1 copy.112
  27.4 0.1 broadcast_add_fusion
  27.6 0.8 reshape.460
  28.5 0.8 broadcast_in_dim.74
  29.4 1.6 scatter_custom_fusion.1
  30.9 0.2 copy.114
  31.1 4.0 scatter_custom_fusion.2
  35.1 1.8 copy.115
  37.0 7.2 %all-to-all-start.2 = ((bf16[16,128,2]{1,2,0:T(2,128)(2,1)}), bf16[16,128,2]{1,2,0:T(2,128)(2,1)S(1)}, u32[]{:S(2)}, u32[]{:S(2)}) async-start(bf16[16,128,2]{1,2,0:T(2,128)(2,1)} %copy.115), calls=%async_computation.2 | async-start | bytes 16384 | tf_op jit(solution)/shard_map/all_to_all | solution.py:96
  44.2 0.1 reshape.454
  44.3 1.3 fusion.50
  45.6 5.6 all-to-all-done.2
  51.2 4.0 all-to-all-start.1
  55.2 13.7 %gather_fusion = bf16[2048,1024]{1,0:T(8,128)(2,1)} fusion(bf16[2048,1024]{1,0:T(8,128)(2,1)} %param.13, s32[2048]{0:T(1024)S(1)} %broadcast_clamp_fusion), kind=kCustom, calls=%fused_computation | custom fusion | bytes 8396800 | tf_op jit(solution)/shard_map/jit(_take)/gather | solution.py:123
  69.0 3.8 broadcast_select_fusion
  72.8 4.3 fusion.98
  77.0 1.6 fusion.96
  78.6 3.4 fusion.34
  82.0 2.6 pad_maximum_fusion
  84.6 7.3 %all-to-all-start.3 = ((bf16[16,136,1024]{2,1,0:T(8,128)(2,1)}), bf16[16,136,1024]{2,1,0:T(8,128)(2,1)}, u32[]{:S(2)}, u32[]{:S(2)}) async-start(bf16[16,136,1024]{2,1,0:T(8,128)(2,1)} %pad_maximum_fusion), calls=%async_computation.3 | async-start | bytes 8912896 | tf_op jit(solution)/shard_map/all_to_all | solution.py:127
  91.9 0.5 all-gather.2.cloned.1.call-start
  92.6 0.1 copy.118
  92.7 53.1 %all-to-all-done.3 = bf16[16,136,1024]{2,1,0:T(8,128)(2,1)} async-done(((bf16[16,136,1024]{2,1,0:T(8,128)(2,1)}), bf16[16,136,1024]{2,1,0:T(8,128)(2,1)}, u32[]{:S(2)}, u32[]{:S(2)}) %all-to-all-start.3) | async-done | bytes 4456480 | tf_op jit(solution)/shard_map/all_to_all | solution.py:127
  145.8 8.8 %gather_fusion.2 = bf16[1024,1024]{1,0:T(8,128)(2,1)} fusion(bf16[2176,1024]{1,0:T(8,128)(2,1)} %bitcast.15, s32[1024]{0:T(1024)S(1)} %broadcast_clamp_fusion.1), kind=kCustom, calls=%fused_computation.2 | custom fusion | bytes 4198400 | tf_op jit(solution)/shard_map/jit(_take)/gather | solution.py:134
  154.6 3.6 gather_fusion.1
  158.3 0.2 convert_reduce_fusion.2
  158.6 2.9 copy_select_fusion
  161.5 1.5 pad_maximum_fusion.1
  163.1 58.9 %all-gather.2.cloned.1.call-done = bf16[32,65,1024]{2,0,1:T(8,128)(2,1)} async-done(((bf16[16,65,1024]{2,0,1:T(8,128)(2,1)}), bf16[32,65,1024]{2,0,1:T(8,128)(2,1)}) %all-gather.2.cloned.1.call-update) | async-done | bytes 4259856 | tf_op jit(solution)/shard_map/all_gather | solution.py:139
  222.0 15.0 %convolution_convert_fusion = bf16[32,65,3,512]{3,1,2,0:T(8,128)(2,1)} fusion(bf16[32,65,1024,1]{2,0,1,3:T(8,128)(2,1)} %bitcast.95, bf16[1024,3,512]{2,0,1:T(8,128)(2,1)S(1)} %copy-done), kind=kOutput, calls=%fused_computation.39 | convolution fusion | flops 6546309120 | bytes 13795328 | tf_op jit(solution)/shard_map/gsd,dcf->gscf/dot_general | solution.py:140
  237.0 13.7 %copy.138 = bf16[32,65,3,512]{1,3,0,2:T(8,128)(2,1)} copy(bf16[32,65,3,512]{3,1,2,0:T(8,128)(2,1)} %convolution_convert_fusion) | data formatting | bytes 12779520 | tf_op jit(solution)/shard_map/reshape | solution.py:34
  250.7 6.3 %fusion.22 = f32[32,8,65,65]{2,3,1,0:T(8,128)S(1)} fusion(bf16[32,65,3,8,64]{1,4,3,0,2:T(8,128)(2,1)} %bitcast.98), kind=kOutput, calls=%fused_computation.50 | convolution fusion | flops 138444800 | bytes 12715008 | tf_op jit(solution)/shard_map/gshe,gthe->ghst/dot_general | solution.py:35
  257.0 5.0 fusion.99
  262.0 6.5 %fusion.32 = bf16[32,8,64,65]{3,2,1,0:T(8,128)(2,1)S(1)} fusion(f32[32,8,65,65]{2,3,1,0:T(8,128)} %get-tuple-element.26, f32[32,8,65]{2,1,0:T(8,128)S(1)} %get-tuple-element.25, bf16[32,65,3,8,64]{1,4,3,0,2:T(8,128)(2,1)} %bitcast.99), kind=kOutput, calls=%fused_computation.60 | convolution fusion | flops 141672960 | bytes 15827968 | tf_op jit(solution)/shard_map/ghst,gthe->gshe/dot_general | solution.py:39
  268.5 4.4 convolution_convert_fusion.1
  272.9 0.2 reduce-scatter.2.cloned.1.call-start
  273.1 126.7 %all-reduce.2.cloned.1.call-done = bf16[32,65,1024]{2,1,0:T(8,128)(2,1)} async-done(((bf16[32,65,1024]{2,1,0:T(8,128)(2,1)}), bf16[32,65,1024]{2,1,0:T(8,128)(2,1)}) %all-reduce.2.cloned.1.call-update) | async-done | bytes 4259856 | tf_op jit(solution)/shard_map/psum | solution.py:143
  399.8 6.4 %fusion.13 = f32[32,65]{1,0:T(8,128)S(1)} fusion(bf16[32,65,1024]{2,1,0:T(8,128)(2,1)} %all-reduce.2.cloned.1.call-done, bf16[32,65,1024]{2,0,1:T(8,128)(2,1)} %all-gather.2.cloned.1.call-done), kind=kLoop, calls=%fused_computation.36 | loop fusion | flops 8517600 | bytes 8528000 | tf_op jit(solution)/shard_map/reduce_sum | solution.py:18
  406.2 5.7 %multiply_reduce_fusion = f32[32,65]{1,0:T(8,128)S(1)} fusion(bf16[32,65,1024]{2,1,0:T(8,128)(2,1)S(1)} %copy-done.2, f32[32,65]{1,0:T(8,128)S(1)} %broadcast_multiply_fusion, bf16[32,65,1024]{2,0,1:T(8,128)(2,1)} %all-gather.2.cloned.1.call-done), kind=kLoop, calls=%fused_computation.30 | loop fusion | flops 12777440 | bytes 8536320 | tf_op jit(solution)/shard_map/reduce_sum | solution.py:20
  411.9 3.5 multiply_convert_fusion
  415.5 17.1 %convert_reduce_fusion.1 = (u32[65,2048]{1,0:T(8,128)S(1)}, u32[65,2048]{1,0:T(8,128)S(1)}, f32[32,65,2048]{2,1,0:T(8,128)}) fusion(bf16[32,65,1024]{2,1,0:T(8,128)(2,1)S(1)} %multiply_convert_fusion, bf16[1024,2048]{1,0:T(8,128)(2,1)S(1)} %copy-done.10), kind=kOutput, calls=%fused_computation.15 | convolution fusion | flops 8770744320 | bytes 26558464 | tf_op jit(solution)/shard_map/gsd,df->gsf/dot_general | solution.py:146
  432.6 54.0 %fusion.27 = bf16[32,65,1024]{2,1,0:T(8,128)(2,1)} fusion(bf16[2048,1024]{1,0:T(8,128)(2,1)S(1)} %copy-done.11, f32[32,65,2048]{2,1,0:T(8,128)} %get-tuple-element.27, u32[65,2048]{1,0:T(8,128)S(1)} %get-tuple-element.6, u32[65,2048]{1,0:T(8,128)S(1)} %get-tuple-element.5), kind=kOutput, calls=%fused_computation.59 | convolution fusion | flops 9015951360 | bytes 26558464 | tf_op jit(solution)/shard_map/gsf,fd->gsd/dot_general | solution.py:150
  486.6 63.6 %reduce-scatter.2.cloned.1.call-done = bf16[16,65,1024]{2,1,0:T(8,128)(2,1)} async-done(((bf16[32,65,1024]{2,1,0:T(8,128)(2,1)}), bf16[16,65,1024]{2,1,0:T(8,128)(2,1)}) %reduce-scatter.2.cloned.1.call-update) | async-done | bytes 2129936 | tf_op jit(solution)/shard_map/reduce_scatter | solution.py:149
  550.3 3.3 fusion.21
  553.5 3.5 multiply_reduce_fusion.2
  557.0 2.4 multiply_convert_fusion.1
  559.5 2.5 copy.128
  (71 shorter events, 1.1 us)
Async XLA Ops:
  6.5 215.5 %copy-start = (bf16[1024,3,512]{2,0,1:T(8,128)(2,1)S(1)}, bf16[1024,3,512]{2,0,1:T(8,128)(2,1)}, u32[]{:S(2)}) copy-start(bf16[1024,3,512]{2,0,1:T(8,128)(2,1)} %param.18) | copy-start | bytes 9437188
  11.3 25.7 %all-to-all-start = ((bf16[16,8,4]{1,2,0:T(4,128)(2,1)}), bf16[16,8,4]{1,2,0:T(4,128)(2,1)S(1)}, u32[]{:S(2)}, u32[]{:S(2)}) async-start(bf16[16,8,4]{1,2,0:T(4,128)(2,1)} %copy.110), calls=%async_computation | async-start | bytes 32768 | tf_op jit(solution)/shard_map/all_to_all | solution.py:89
  37.0 14.2 %all-to-all-start.2 = ((bf16[16,128,2]{1,2,0:T(2,128)(2,1)}), bf16[16,128,2]{1,2,0:T(2,128)(2,1)S(1)}, u32[]{:S(2)}, u32[]{:S(2)}) async-start(bf16[16,128,2]{1,2,0:T(2,128)(2,1)} %copy.115), calls=%async_computation.2 | async-start | bytes 16384 | tf_op jit(solution)/shard_map/all_to_all | solution.py:96
  51.2 21.6 %all-to-all-start.1 = ((bf16[16,8,1024]{2,1,0:T(8,128)(2,1)}), bf16[16,8,1024]{2,1,0:T(8,128)(2,1)S(1)}, u32[]{:S(2)}, u32[]{:S(2)}) async-start(bf16[16,8,1024]{2,1,0:T(8,128)(2,1)} %bitcast.3), calls=%async_computation.1 | async-start | bytes 524288 | tf_op jit(solution)/shard_map/all_to_all | solution.py:82
  72.8 9.2 %copy-start.5 = (bf16[16,128,1024]{2,1,0:T(8,128)(2,1)S(1)}, bf16[16,128,1024]{2,1,0:T(8,128)(2,1)}, u32[]{:S(2)}) copy-start(bf16[16,128,1024]{2,1,0:T(8,128)(2,1)} %broadcast_select_fusion) | copy-start | bytes 12582916
  84.6 61.2 %all-to-all-start.3 = ((bf16[16,136,1024]{2,1,0:T(8,128)(2,1)}), bf16[16,136,1024]{2,1,0:T(8,128)(2,1)}, u32[]{:S(2)}, u32[]{:S(2)}) async-start(bf16[16,136,1024]{2,1,0:T(8,128)(2,1)} %pad_maximum_fusion), calls=%async_computation.3 | async-start | bytes 8912896 | tf_op jit(solution)/shard_map/all_to_all | solution.py:127
  91.9 130.1 %all-gather.2.cloned.1.call-start = ((), (), s32[]{:S(2)}) async-start(), calls=%async_computation.5 | async-start | bytes 6389760 | tf_op jit(solution)/shard_map/all_gather | solution.py:139
  145.8 12.8 %copy-start.7 = (bf16[16,1024]{1,0:T(8,128)(2,1)S(1)}, bf16[16,1024]{1,0:T(8,128)(2,1)}, u32[]{:S(2)}) copy-start(bf16[16,1024]{1,0:T(8,128)(2,1)} %param.12) | copy-start | bytes 98308
  163.1 236.7 %all-reduce.2.cloned.1.call-start = ((), (), s32[]{:S(2)}) async-start(), calls=%async_computation.6 | async-start | bytes 9437184 | tf_op jit(solution)/shard_map/psum | solution.py:143
  262.0 6.5 %copy-start.6 = (bf16[512,1024]{1,0:T(8,128)(2,1)S(1)}, bf16[512,1024]{1,0:T(8,128)(2,1)}, u32[]{:S(2)}) copy-start(bf16[512,1024]{1,0:T(8,128)(2,1)} %param.19) | copy-start | bytes 3145732
  272.9 139.0 %slice-start = ((s8[4259840]{0:T(1024)(128)(4,1)}), s8[65536]{0:T(1024)(128)(4,1)S(1)}, s32[]{:S(2)}) async-start(s8[4259840]{0:T(1024)(128)(4,1)} %bitcast.96), calls=%async_computation.8 | async-start | bytes 131072
  272.9 139.0 %copy-start.8 = (f32[1024]{0:T(1024)S(1)}, f32[1024]{0:T(1024)}, u32[]{:S(2)}) copy-start(f32[1024]{0:T(1024)} %param.22) | copy-start | bytes 12292
  272.9 277.4 %reduce-scatter.2.cloned.1.call-start = ((), (), s32[]{:S(2)}) async-start(), calls=%async_computation.7 | async-start | bytes 7077888 | tf_op jit(solution)/shard_map/reduce_scatter | solution.py:149
  399.8 6.4 %copy-start.2 = (bf16[32,65,1024]{2,1,0:T(8,128)(2,1)S(1)}, bf16[32,65,1024]{2,1,0:T(8,128)(2,1)}, u32[]{:S(2)}) copy-start(bf16[32,65,1024]{2,1,0:T(8,128)(2,1)} %all-reduce.2.cloned.1.call-done) | copy-start | bytes 12779524
  406.2 5.8 %slice-start.1 = ((s8[4259840]{0:T(1024)(128)(4,1)}), s8[4194304]{0:T(1024)(128)(4,1)S(1)}, s32[]{:S(2)}) async-start(s8[4259840]{0:T(1024)(128)(4,1)} %bitcast.96), calls=%async_computation.9 | async-start | bytes 8388608
  406.2 9.3 %copy-start.10 = (bf16[1024,2048]{1,0:T(8,128)(2,1)S(1)}, bf16[1024,2048]{1,0:T(8,128)(2,1)}, u32[]{:S(2)}) copy-start(bf16[1024,2048]{1,0:T(8,128)(2,1)} %param.20) | copy-start | bytes 12582916
  415.5 17.1 %copy-start.3 = (bf16[32,65,1024]{2,1,0:T(8,128)(2,1)}, bf16[32,65,1024]{2,1,0:T(8,128)(2,1)S(1)}, u32[]{:S(2)}) copy-start(bf16[32,65,1024]{2,1,0:T(8,128)(2,1)S(1)} %multiply_convert_fusion) | copy-start | bytes 12779524
  415.5 17.1 %copy-start.11 = (bf16[2048,1024]{1,0:T(8,128)(2,1)S(1)}, bf16[2048,1024]{1,0:T(8,128)(2,1)}, u32[]{:S(2)}) copy-start(bf16[2048,1024]{1,0:T(8,128)(2,1)} %param.21) | copy-start | bytes 12582916
  486.6 70.4 %copy-start.9 = (f32[1024]{0:T(1024)S(1)}, f32[1024]{0:T(1024)}, u32[]{:S(2)}) copy-start(f32[1024]{0:T(1024)} %param.23) | copy-start | bytes 12292
  486.6 75.3 %copy-start.1 = (bf16[1024,3,512]{2,0,1:T(8,128)(2,1)S(1)}, bf16[1024,3,512]{2,0,1:T(8,128)(2,1)}, u32[]{:S(2)}) copy-start(bf16[1024,3,512]{2,0,1:T(8,128)(2,1)} %param.18) | copy-start | bytes 9437188
  550.3 6.8 %copy-start.4 = (bf16[16,65,1024]{2,1,0:T(8,128)(2,1)S(1)}, bf16[16,65,1024]{2,1,0:T(8,128)(2,1)}, u32[]{:S(2)}) copy-start(bf16[16,65,1024]{2,1,0:T(8,128)(2,1)} %reduce-scatter.2.cloned.1.call-done) | copy-start | bytes 6389764
Sparse Core Ops, SparseCore 0:
  163.2 58.7 all-gather.1
  273.0 126.7 all-reduce.1
  486.7 63.4 reduce-scatter.1
where the time goes:
time: 576 us; the launch traced here: 569 us
  waiting for transfers between devices  308 us (53%)
  matrix products  112 us (19%)
  local copies, waits for them, and re-layouts  56.8 us (10%)
  other arithmetic  50.4 us (9%)
  starting transfers between devices  27.7 us (5%)
  between operations  13.8 us (2%)
    psum x1, waiting for transfers between devices, on_device(): attn = lax.psum(partial_attn.astype(jnp.bfloat16), 'tp').astype(jnp.float32)  127 us
    reduce_scatter x1, waiting for transfers between devices, on_device(): lax.psum_scatter(jnp.einsum('gsf,fd->gsd', active, w_down, preferred_elem...  63.6 us
    all_gather x1, waiting for transfers between devices, on_device(): all_tokens = lax.all_gather(tokens, 'tp', axis=0, tiled=True)  58.9 us
    dot_general x1, matrix products, on_device(): jnp.einsum('gsf,fd->gsd', active, w_down, preferred_element_type=f32)  54 us
    all_to_all x1, waiting for transfers between devices, on_device(): lax.all_to_all(reply, 'index', split_axis=0, concat_axis=0, tiled=True)  53.1 us
    dot_general x1, matrix products, on_device(): jnp.einsum('gsd,df->gsf', hidden_all, w_up, preferred_element_type=f32)  17.1 us
    dot_general x1, matrix products, on_device(): jnp.einsum('gsd,dcf->gscf', all_tokens, w_qkv, preferred_element_type=f32)  15 us
    reshape x1, local copies, waits for them, and re-layouts, attend(): shaped = qkv.reshape(lists, S, 3, head_count, HD)  13.7 us
  transfers between devices with their start and end apart: 7, of which 5 were waited for; matrix products, arithmetic and copies ran while one was open for 6% of the time, Pallas kernels for 0%

commit v1 on v0

v1 whole, which is shorter than its diff:
```python
import math

import jax
import jax.numpy as jnp
from jax import lax
from jax.experimental import pallas as pl
from jax.experimental.pallas import tpu as pltpu
from jax.sharding import PartitionSpec as P

NT = (((1,), (1,)), ((), ()))
MESH = pl.DeviceIdType.MESH
bf16 = jnp.bfloat16
f32 = jnp.float32
D = 1024
Q_DEV = 16
PASS_DEV = 2048
N_C = 1024
N_TOK = 1040

def gelu(x):
    ax=jnp.abs(x)
    t=1.0/(1.0+(0.3275911*math.sqrt(0.5))*ax)
    e=jnp.exp2((-0.5/math.log(2.0))*(x*x))
    p=0.5*0.254829592+t*(0.5*-0.284496736+t*(0.5*1.421413741+t*(0.5*-1.453152027+t*(0.5*1.061405429))))
    return jnp.maximum(x,0.0)-ax*(p*t*e)

def norm(v,g):
    c=v-jnp.mean(v,-1,keepdims=True)
    var=jnp.mean(c*c,-1,keepdims=True)
    return c*lax.rsqrt(var+1e-5)*g

def layer_kernel(tok,wq0,wq1,wo0,wo1,wu0,wu1,wd0,wd1,g1,g2,out,
                 wq,wo,wu,wd,q,k,v,kl,vl,ctx,ctxl,acc,sems):
    cps=[]
    for n,(dst,a,b) in enumerate(((wq,wq0,wq1),(wo,wo0,wo1),(wu,wu0,wu1),(wd,wd0,wd1))):
        for s,src in enumerate((a,b)):
            c=pltpu.make_async_copy(src,dst.at[s],sems.at[n,s]); c.start(); cps.append(c)
    for i in range(2):
        cps[i].wait()
        def qkv_step(n,carry):
            col=pl.ds(pl.multiple_of(n*256,256),256)
            ocol=pl.ds(pl.multiple_of(i*512+n*256,256),256)
            for j,ref in enumerate((q,k,v)):
                r=jnp.dot(tok[...],wq[i,j,:,col],preferred_element_type=f32)
                if j==0: r=r*0.125
                ref[:,ocol]=r.astype(bf16)
            return carry
        lax.fori_loop(0,2,qkv_step,0)
    kl[...]=k[N_C:,:].astype(f32); vl[...]=v[N_C:,:].astype(f32)
    ctxl[...]=jnp.zeros_like(ctxl)
    lane=lax.broadcasted_iota(jnp.int32,(64,256),1)//64
    ones_bd=(lax.broadcasted_iota(jnp.int32,(256,256),0)//64==lax.broadcasted_iota(jnp.int32,(256,256),1)//64).astype(bf16)
    low=lax.broadcasted_iota(jnp.int32,(80,128),1)<64
    rowid=lax.broadcasted_iota(jnp.int32,(16,256),0)
    def bd(x):
        return jnp.concatenate([jnp.where(lane==h,x,jnp.zeros_like(x)) for h in range(4)],0)
    def att(g,carry):
        rows=pl.ds(pl.multiple_of(g*64,64),64)
        es=[];els=[];
        for j in range(4):
            cs=slice(j*256,(j+1)*256)
            Q=jnp.concatenate([q[rows,cs],q[N_C:,cs]],0)
            klb=jnp.broadcast_to(kl[pl.ds(g,1),cs],(64,256)).astype(bf16)
            S=lax.dot_general(Q,bd(k[rows,cs]),NT,preferred_element_type=f32)
            SL=lax.dot_general(Q,bd(klb),NT,preferred_element_type=f32)
            ms=[]
            for b in range(2):
                X=S[:,b*128:(b+1)*128]
                mA=jnp.max(jnp.where(low,X,-jnp.inf),1,keepdims=True)
                mB=jnp.max(jnp.where(low,-jnp.inf,X),1,keepdims=True)
                ms.append(jnp.where(low,mA,mB))
            m=jnp.maximum(jnp.concatenate(ms,1),SL)
            es.append(jnp.exp(S-m).astype(bf16)); els.append(jnp.exp(SL-m))
        den=jnp.dot(jnp.concatenate(es,0),ones_bd,preferred_element_type=f32)
        for j in range(4):
            cs=slice(j*256,(j+1)*256)
            pv=jnp.dot(es[j],bd(v[rows,cs]),preferred_element_type=f32)
            c=(pv+els[j]*vl[pl.ds(g,1),cs])/(den[j*80:(j+1)*80]+els[j])
            ctx[rows,cs]=c[:64].astype(bf16)
            ctxl[:,cs]+=jnp.where(rowid==g,c[64:],0.0)
        return carry
    lax.fori_loop(0,16,att,0)
    ctx[N_C:,:]=ctxl[...].astype(bf16)
    cps[2].wait(); cps[3].wait()
    def outp(rows,n):
        a=jnp.dot(ctx[rows,:512],wo[0],preferred_element_type=f32)+jnp.dot(ctx[rows,512:],wo[1],preferred_element_type=f32)
        return norm(tok[rows,:].astype(f32)+a,g1[...]).astype(bf16).astype(f32)
    def put(g,y):
        for c in range(8): acc[c,pl.ds(16+g,64,stride=16),:]=y[:,c*128:(c+1)*128]
    def outc(i,carry):
        h=outp(pl.ds(pl.multiple_of(i*256,256),256),256)
        for l in range(4):
            put(i*4+l,h[l*64:(l+1)*64])
        return carry
    lax.fori_loop(0,3,outc,0)
    h=outp(slice(768,1040),272)
    for l in range(4):
        put(12+l,h[l*64:(l+1)*64])
    for c in range(8): acc[c,0:16,:]=h[256:,c*128:(c+1)*128]
    for c in cps[4:]: c.wait()
    def ffn(r,carry):
        rows=pl.ds(pl.multiple_of(r*208,16),208)
        t=jnp.concatenate([acc[c,rows,:] for c in range(8)],1)
        x=t.astype(bf16)
        acts=[]
        for i in range(2):
            for n in range(4):
                u=jnp.dot(x,wu[i,:,n*512:(n+1)*512],preferred_element_type=f32)
                acts.append(gelu(u).astype(bf16))
        for i in range(2):
            t=t+jnp.dot(jnp.concatenate(acts[i*4:(i+1)*4],1),wd[i],preferred_element_type=f32)
        out[rows,:]=norm(t,g2[...]).astype(bf16)
        return carry
    lax.fori_loop(0,5,ffn,0)

def layer(tok,wq0,wq1,wo0,wo1,wu0,wu1,wd0,wd1,g1,g2):
    V=pl.BlockSpec(memory_space=pltpu.VMEM); A=pl.BlockSpec(memory_space=pl.ANY)
    o=pl.pallas_call(layer_kernel,out_shape=jax.ShapeDtypeStruct((N_TOK,D),bf16),
        in_specs=[V]+[A]*8+[V,V],out_specs=V,
        scratch_shapes=[pltpu.VMEM((2,3,1024,512),bf16),pltpu.VMEM((2,512,1024),bf16),pltpu.VMEM((2,1024,2048),bf16),pltpu.VMEM((2,2048,1024),bf16),
          pltpu.VMEM((N_TOK,D),bf16),pltpu.VMEM((N_TOK,D),bf16),pltpu.VMEM((N_TOK,D),bf16),pltpu.VMEM((16,D),f32),pltpu.VMEM((16,D),f32),
          pltpu.VMEM((N_TOK,D),bf16),pltpu.VMEM((16,D),f32),pltpu.VMEM((8,N_TOK,128),f32),pltpu.SemaphoreType.DMA((4,2))],
        compiler_params=pltpu.CompilerParams(vmem_limit_bytes=60*2**20),name="layer",
        cost_estimate=pl.CostEstimate(flops=2*1040*12*2**20,bytes_accessed=30*2**20,transcendentals=8*2**20))(tok,wq0,wq1,wo0,wo1,wu0,wu1,wd0,wd1,g1,g2)
    return jnp.transpose(o.reshape(65,16,D),(1,0,2))

ORDER = ((2, 1), (2, 0), (1, 1), (3, 1), (1, 0), (3, 0), (0, 1), (0, 0))
UNITS = ((0, 0), (0, 1), (0, 2), (1, 0), (2, 0), (3, 0))
ROWS = (128, 64, 128, 256)


def inverse(k):
    return ((4 - k // 4) % 4) * 4 + k % 4


def front_kernel(
    own,
    pay,
    qry,
    psg_in,
    wq_i,
    wo_i,
    wu_i,
    wd_i,
    tok,
    wq_o,
    wo_o,
    wu_o,
    wd_o,
    psg,
    qall,
    msg,
    got,
    hot,
    reply,
    back,
    codes,
    frows,
    score,
    pool,
    prow,
    flatcol,
    psem,
    qsem,
    msem,
    rsem,
    osem,
    wsend,
    wrecv,
):
    idx = lax.axis_index("index")
    z = lax.axis_index("rep")
    t = lax.axis_index("tp")
    y, xh, c = idx // 4, (idx // 2) % 2, idx % 2

    def peer(k):
        dy, dx, dc = k // 4, (k // 2) % 2, k % 2
        return (((y + dy) % 4) * 4 + ((xh + dx) % 2) * 2 + (c + dc) % 2, z, (t + dx) % 2)

    partner = (idx, z, 1 - t)
    z_up = (idx, (z + 1) % 4, t)
    z_down = (idx, (z + 3) % 4, t)
    barrier = pltpu.get_barrier_semaphore()
    for device in [peer(k) for k in range(1, 16)] + [partner, z_up, z_down]:
        pl.semaphore_signal(barrier, inc=1, device_id=device, device_id_type=MESH)
    load = pltpu.make_async_copy(psg_in, psg, psem)
    load.start()

    owner = own[...]
    rel = (((owner >> 2) - y) & 3) * 4 + (((owner >> 1) & 1) ^ xh) * 2 + ((owner & 1) ^ c)
    rel = jnp.where(owner < 0, -1, rel).astype(f32)
    sub16 = lax.broadcasted_iota(jnp.int32, (16, 128), 0).astype(f32)
    marks = [jnp.where(rel[r : r + 1, :] == sub16, 1.0, 0.0) for r in range(16)]
    onehot = jnp.concatenate(marks, 0)
    onehot16 = onehot.astype(bf16)
    row128 = lax.broadcasted_iota(jnp.int32, (128, 128), 0)
    col128 = lax.broadcasted_iota(jnp.int32, (128, 128), 1)
    same = (row128 // 64) == (col128 // 64)
    earlier = jnp.where(same & (row128 < col128), 1.0, 0.0).astype(bf16)
    block = jnp.where(same, 1.0, 0.0).astype(bf16)
    row256 = lax.broadcasted_iota(jnp.int32, (256, 256), 0)
    col256 = lax.broadcasted_iota(jnp.int32, (256, 256), 1)
    above = jnp.where(((row256 % 16) == (col256 % 16)) & (col256 < row256 - row256 % 16), 1.0, 0.0)
    lists_before = jnp.dot(above.astype(bf16), onehot16, preferred_element_type=f32).astype(bf16)
    count = jnp.dot(onehot16, earlier, preferred_element_type=f32)
    count = count + jnp.dot(lists_before, block, preferred_element_type=f32)
    slot = jnp.sum((onehot * count).reshape(16, 16, 128), 1)

    lane16 = lax.broadcasted_iota(jnp.int32, (16, 128), 1)
    target = jnp.where(lane16 < 64, slot, slot + 128.0)
    high = (pay[...] >> 5).astype(f32)
    low = (pay[...] & 31).astype(f32)
    sub256 = lax.broadcasted_iota(jnp.int32, (256, 128), 0).astype(f32)
    pad = jnp.zeros((96, 128), f32)
    table = jnp.zeros((256, 128), f32)
    for r in range(16):
        here = jnp.where(target[r : r + 1, :] == sub256, 1.0, 0.0).astype(bf16)
        digit = jnp.concatenate([marks[r] * high[r : r + 1, :], marks[r] * low[r : r + 1, :], pad], 0)
        table = table + lax.dot_general(here, digit.astype(bf16), NT, preferred_element_type=f32)
    table = jnp.transpose(table)
    table = table[:16] * 32.0 + table[16:32]
    for k in range(16):
        msg[k] = jnp.broadcast_to(table[k : k + 1, :], (8, 256))
    got[0] = msg[0]
    qall[0] = qry[...]

    pl.semaphore_wait(barrier, 18)

    w_in = (wq_i, wo_i, wu_i, wd_i)
    w_out = (wq_o, wo_o, wu_o, wd_o)

    def share(refs, unit, zz, cc, half=None):
        n, j = UNITS[unit]
        rows = ROWS[n]
        start = (zz * 2 + cc) * rows
        if half is not None:
            rows = rows // 2
            start = start + half * rows
        part = pl.ds(pl.multiple_of(start, 32), rows)
        return refs[n].at[j, part, :] if n == 0 else refs[n].at[part, :]

    def push(src, dst, unit, s, device):
        copy = pltpu.make_async_remote_copy(
            src_ref=src,
            dst_ref=dst,
            send_sem=wsend.at[unit, s],
            recv_sem=wrecv.at[unit, s],
            device_id=device,
            device_id_type=MESH,
        )
        copy.start()
        return copy

    started = {}
    for u in range(6):
        started[u, 0] = push(share(w_in, u, z, c), share(w_out, u, z, c), u, 0, partner)

    def relay(u, stage):
        def put(s, zz, half, device):
            ref = share(w_out, u, zz, c, half)
            started[u, s] = push(ref, ref, u, s, device)

        zm, zp, zo = (z + 3) % 4, (z + 1) % 4, (z + 2) % 4
        if stage == 0:
            started[u, 0].wait_recv()
            put(1, z, None, z_up)
            put(2, z, None, z_down)
            put(5, z, None, peer(1))
        elif stage == 1:
            started[u, 1].wait_recv()
            put(3, zm, 0, z_up)
            put(6, zm, None, peer(1))
            started[u, 2].wait_recv()
            put(4, zp, 1, z_down)
            put(7, zp, None, peer(1))
        else:
            started[u, 3].wait_recv()
            started[u, 4].wait_recv()
            put(8, zo, None, peer(1))

    def remote(src, dst, sems, k):
        copy = pltpu.make_async_remote_copy(
            src_ref=src,
            dst_ref=dst,
            send_sem=sems.at[0, k],
            recv_sem=sems.at[1, inverse(k)],
            device_id=peer(k),
            device_id_type=MESH,
        )
        copy.start()
        return copy

    steps = [dy * 4 + dx * 2 for dy, dx in ORDER]
    pairs = [k for first in steps for k in (first, first + 1) if k]
    m_copy = {k: remote(msg.at[k], got.at[inverse(k)], msem, k) for k in pairs}
    q_copy = {k: remote(qry, qall.at[inverse(k)], qsem, k) for k in pairs}

    flat = jnp.where(lane16 < 64, rel * 128.0 + slot, rel * 16.0 + slot)
    eye = row128 == col128
    for r in range(16):
        column = jnp.sum(jnp.where(eye[:64], flat[r : r + 1, :], 0.0), 1, keepdims=True)
        flatcol[r * 64 : (r + 1) * 64, :] = jnp.broadcast_to(column, (64, 128))

    load.wait()
    r_copy = {}
    lanes = lax.broadcasted_iota(jnp.int32, (128, 2048), 1).astype(f32)
    for number, first in enumerate(steps):
        for k in (first, first + 1):
            if k:
                m_copy[inverse(k)].wait_recv()
            column = jnp.sum(jnp.where(eye, got[k, 0:1, 0:128], 0.0), 1, keepdims=True)
            hot[(k % 2) * 128 : (k % 2 + 1) * 128, :] = jnp.where(column == lanes, 1.0, 0.0).astype(bf16)

        def gather(n, carry, first=first):
            cols = pl.ds(pl.multiple_of(n * 256, 256), 256)
            rows = jnp.dot(hot[...], psg[:, cols], preferred_element_type=f32).astype(bf16)
            if first:
                reply[first, :, cols] = rows[:128]
            else:
                back[0, :, cols] = rows[:128]
            reply[first + 1, :, cols] = rows[128:]
            return carry

        lax.fori_loop(0, 4, gather, 0)
        for k in (first, first + 1):
            if k:
                r_copy[k] = remote(reply.at[k], back.at[inverse(k)], rsem, k)
        if number == 3:
            relay(0, 0)
        elif number == 5:
            relay(1, 0)

    relay(2, 0)
    relay(0, 1)
    eye8 = eye[:8]
    for k in range(16):
        column = jnp.sum(jnp.where(eye8, got[k, 0:1, 128:256], 0.0), 1, keepdims=True)
        codes[k * 8 : (k + 1) * 8, :] = jnp.broadcast_to(column, (8, 128))
    for k in pairs:
        q_copy[k].wait_recv()
    code = codes[...].astype(jnp.int32) - 1
    slot_row = lax.broadcasted_iota(jnp.int32, (128, 256), 0)
    slot_col = lax.broadcasted_iota(jnp.int32, (128, 256), 1)
    code2 = jnp.concatenate([code, code], 1)
    pick = (slot_col == (slot_row // 8) * 16 + (code2 >> 2)) & (code2 >= 0)
    chosen = jnp.where(pick, 1.0, 0.0).astype(bf16)
    queries_all = qall[...].reshape(256, D)
    frows[...] = jnp.dot(chosen, queries_all, preferred_element_type=f32).astype(bf16)
    cluster = code[:, 0:1] & 3

    def score_step(n, carry):
        rows = pl.ds(pl.multiple_of(n * 512, 512), 512)
        s = lax.dot_general(frows[...], psg[rows, :], NT, preferred_element_type=f32)
        score[:, rows] = jnp.where(cluster == n, s * (D ** (-0.5)), -1e30)
        return carry

    lax.fori_loop(0, 4, score_step, 0)
    relay(3, 0)
    relay(1, 1)
    peak = jnp.max(score[...], 1, keepdims=True)
    expo = jnp.exp(score[...] - peak)
    weights = (expo / jnp.sum(expo, 1, keepdims=True)).astype(bf16)
    pooled = jnp.dot(weights, psg[...], preferred_element_type=f32)
    for k in range(16):
        rows = jnp.concatenate([pooled[k * 8 : (k + 1) * 8], jnp.zeros((8, D), f32)], 0).astype(bf16)
        if k:
            pool[k] = rows
        else:
            prow[0] = rows
    p_copy = {k: remote(pool.at[k], prow.at[inverse(k)], osem, k) for k in pairs}

    def assemble(dy, fresh):
        for k in range(dy * 4, dy * 4 + 4):
            if k:
                r_copy[inverse(k)].wait_recv()
        wide = (lax.broadcasted_iota(jnp.int32, (256, 512), 1) + dy * 512).astype(f32)

        def part(n, carry):
            rows = pl.ds(pl.multiple_of(n * 256, 256), 256)
            place = jnp.concatenate([flatcol[rows, :]] * 4, 1)
            mark = jnp.where(place == wide, 1.0, 0.0).astype(bf16)
            values = back[dy * 4 : dy * 4 + 4].reshape(512, D)
            found = jnp.dot(mark, values, preferred_element_type=f32).astype(bf16)
            tok[rows, :] = found if fresh else tok[rows, :] + found
            return carry

        lax.fori_loop(0, 4, part, 0)

    relay(2, 1)
    relay(0, 2)
    relay(4, 0)
    relay(1, 2)
    relay(3, 1)
    relay(2, 2)
    assemble(0, True)
    relay(3, 2)
    relay(5, 0)
    relay(4, 1)
    assemble(2, False)
    relay(4, 2)
    relay(5, 1)
    for k in pairs:
        p_copy[k].wait_recv()
    wide = lax.broadcasted_iota(jnp.int32, (16, 256), 1).astype(f32)
    mix = jnp.zeros((16, 256), f32)
    for j in range(4):
        mix = mix + jnp.where(flat[:, 64 + j : 65 + j] == wide, 1.0, 0.0)
    summed = jnp.dot(mix.astype(bf16), prow[...].reshape(256, D), preferred_element_type=f32)
    tok[N_C:, :] = (qry[...].astype(f32) + summed * 0.25).astype(bf16)
    assemble(1, False)
    assemble(3, False)
    relay(5, 2)
    for u in range(6):
        for s in range(5, 9):
            started[u, s].wait_recv()
    for copies in (m_copy, q_copy, r_copy, p_copy, started):
        for copy in copies.values():
            copy.wait_send()


def front(own, pay, qry, passages, wq, wo, wu, wd):
    vmem = pl.BlockSpec(memory_space=pltpu.VMEM)
    hbm = pl.BlockSpec(memory_space=pl.ANY)
    weights = [jax.ShapeDtypeStruct(w.shape, bf16) for w in (wq, wo, wu, wd)]
    dma = pltpu.SemaphoreType.DMA
    return pl.pallas_call(
        front_kernel,
        out_shape=[jax.ShapeDtypeStruct((N_TOK, D), bf16)] + weights,
        in_specs=[vmem, vmem, vmem] + [hbm] * 5,
        out_specs=[vmem] + [hbm] * 4,
        scratch_shapes=[
            pltpu.VMEM((PASS_DEV, D), bf16),
            pltpu.VMEM((16, 16, D), bf16),
            pltpu.VMEM((16, 8, 256), f32),
            pltpu.VMEM((16, 8, 256), f32),
            pltpu.VMEM((256, 2048), bf16),
            pltpu.VMEM((16, 128, D), bf16),
            pltpu.VMEM((16, 128, D), bf16),
            pltpu.VMEM((128, 128), f32),
            pltpu.VMEM((128, D), bf16),
            pltpu.VMEM((128, PASS_DEV), f32),
            pltpu.VMEM((16, 16, D), bf16),
            pltpu.VMEM((16, 16, D), bf16),
            pltpu.VMEM((N_C, 128), f32),
            dma(()),
            dma((2, 16)),
            dma((2, 16)),
            dma((2, 16)),
            dma((2, 16)),
            dma((6, 9)),
            dma((6, 9)),
        ],
        compiler_params=pltpu.CompilerParams(
            collective_id=0, has_side_effects=True, vmem_limit_bytes=56 * 2**20
        ),
        cost_estimate=pl.CostEstimate(flops=2**34, bytes_accessed=50 * 2**20, transcendentals=0),
        name="front",
    )(own, pay, qry, passages, wq, wo, wu, wd)


def on_device(
    queries,
    passages,
    probe_owner,
    probe_cluster,
    pair_owner,
    pair_row,
    w_qkv,
    w_out,
    w_up,
    w_down,
    gain_one,
    gain_two,
):
    blank = jnp.full((Q_DEV, 60), -1, jnp.int32)
    own = jnp.concatenate([pair_owner[:, :, 0], probe_owner, blank], 1)
    code = 1 + jnp.arange(Q_DEV, dtype=jnp.int32)[:, None] * 4 + probe_cluster
    pay = jnp.concatenate([pair_row, code, blank * 0], 1)
    wq = jnp.transpose(w_qkv, (1, 0, 2))
    tok, wq1, wo1, wu1, wd1 = front(own, pay, queries, passages, wq, w_out, w_up, w_down)
    return layer(
        tok, wq, wq1, w_out, wo1, w_up, wu1, w_down, wd1, gain_one[None, :], gain_two[None, :]
    )


def solution(mesh):
    rows = P(("index", "rep", "tp"), None)
    lists = P(("index", "rep", "tp"), None, None)
    in_specs = (
        rows,
        P("index", None),
        rows,
        rows,
        lists,
        rows,
        P(None, None, "tp"),
        P("tp", None),
        P(None, "tp"),
        P("tp", None),
        P(),
        P(),
    )
    return jax.shard_map(
        on_device, mesh=mesh, in_specs=in_specs, out_specs=lists, check_vma=False
    )
```

time: 576 us -> 156 us (0.27); the launches traced: 569 us -> 156 us
  waiting for transfers between devices: 308 us -> 0 us
  Pallas kernels: 0 us -> 152 us
  matrix products: 112 us -> 0 us
  local copies, waits for them, and re-layouts: 56.8 us -> 1.67 us
  other arithmetic: 50.4 us -> 1.47 us
  starting transfers between devices: 27.7 us -> 0 us
  between operations: 13.8 us -> 0.17 us
    pallas_call x0 -> x2, Pallas kernels: none -> 152 us  [the longest x1 97.9 us: front(): pl.pallas_call(front_kernel, out_shape=[jax.ShapeDtypeStruct((N_TOK, D),...]
    psum x1 -> x0, waiting for transfers between devices: 127 us -> none  [on_device(): attn = lax.psum(partial_attn.astype(jnp.bfloat16), 'tp').astype(jnp.float32)]
    dot_general x9 -> x0, matrix products: 112 us -> none  [the longest x1 54 us: on_device(): jnp.einsum('gsf,fd->gsd', active, w_down, preferred_element_type=f32)]
    reduce_scatter x1 -> x0, waiting for transfers between devices: 63.6 us -> none  [on_device(): lax.psum_scatter(jnp.einsum('gsf,fd->gsd', active, w_down, preferred_elem...]
    all_gather x1 -> x0, waiting for transfers between devices: 58.9 us -> none  [on_device(): all_tokens = lax.all_gather(tokens, 'tp', axis=0, tiled=True)]
    all_to_all x4 -> x0, waiting for transfers between devices: 58.6 us -> none  [the longest x1 53.1 us: on_device(): lax.all_to_all(reply, 'index', split_axis=0, concat_axis=0, tiled=True)]
    all_to_all x4 -> x0, starting transfers between devices: 26.9 us -> none  [the longest x1 8.45 us: on_device(): lax.all_to_all(send_marks.reshape(owner_count, probe_cap, CL_DEV), 'index...]
    gather x4 -> x0, local copies, waits for them, and re-layouts: 26.3 us -> none  [the longest x1 13.7 us: on_device(): fetched = jnp.take(passages, fetch_ids, axis=0)]
  transfers between devices with their start and end apart: 7 -> 0, of which waited for: 5 -> 0; matrix products, arithmetic and copies ran while one was open for 6% -> 0% of each run, Pallas kernels for 0% -> 0%
where the time goes in v1:
time: 156 us
  Pallas kernels  152 us (97%)
  local copies, waits for them, and re-layouts  1.67 us (1%)
    pallas_call x1, Pallas kernels, front(): pl.pallas_call(front_kernel, out_shape=[jax.ShapeDtypeStruct((N_TOK, D),...  97.9 us
    pallas_call x1, Pallas kernels, layer(): pl.pallas_call(layer_kernel, out_shape=jax.ShapeDtypeStruct((N_TOK, D), b...  54.4 us

profile of v1, /device:TPU:1, one launch (start us, length us, event | category | flops | bytes accessed | tf_op | source)
XLA Modules:
  0.0 155.6 jit_solution(5102428321598459112)
XLA Ops:
  0.0 0.1 pad.5.clone
  0.1 0.1 pad.2.clone
  0.2 0.8 copy.15
  0.9 0.8 copy.17
  1.7 0.1 broadcast_add_fusion
  1.8 1.4 add_add_fusion
  3.1 97.9 %front.1 = (bf16[1040,1024]{1,0:T(8,128)(2,1)}, bf16[3,1024,512]{2,1,0:T(8,128)(2,1)}, bf16[512,1024]{1,0:T(8,128)(2,1)}, bf16[1024,2048]{1,0:T(8,128)(2,1)}, bf16[2048,1024]{1,0:T(8,128)(2,1)}) custom-call(s32[16,128]{1,0:T(8,128)} %get-tuple-element.15.own, s32[16,128]{1,0:T(8,128)} %get-tuple-element.16.pay, bf16[16,1024]{1,0:T(8,128)(2,1)} %qry.1, ...), custom_call_target="tpu_custom_call" | custom-call | flops 17179869184 | bytes 52428800 | tf_op jit(solution)/shard_map/front/pallas_call | solution.py:426
  101.0 54.4 %layer.1 = bf16[1040,1024]{1,0:T(8,128)(2,1)} custom-call(bf16[1040,1024]{1,0:T(8,128)(2,1)} %get-tuple-element.10.tok, bf16[3,1024,512]{2,1,0:T(8,128)(2,1)} %bitcast.9, bf16[3,1024,512]{2,1,0:T(8,128)(2,1)} %get-tuple-element.11.wq1, bf16[512,1024]{1,0:T(8,128)(2,1)} %wo0.1, bf16[512,1024]{1,0:T(8,128)(2,1)} %get-tuple-element.12.wo1, ...), custom_call_target="tpu_custom_call" | custom-call | flops 26172456960 | bytes 31457280 | tf_op jit(solution)/shard_map/layer/pallas_call | solution.py:118
  (3 shorter events, 0.0 us)

commit v2 on v1

v2 whole, which is shorter than its diff:
```python
import math

import jax
import jax.numpy as jnp
from jax import lax
from jax.experimental import pallas as pl
from jax.experimental.pallas import tpu as pltpu
from jax.sharding import PartitionSpec as P

NT = (((1,), (1,)), ((), ()))
MESH = pl.DeviceIdType.MESH
bf16 = jnp.bfloat16
f32 = jnp.float32
D = 1024
Q_DEV = 16
PASS_DEV = 2048
N_C = 1024
N_TOK = 1040

def gelu(x):
    ax=jnp.abs(x)
    t=1.0/(1.0+(0.3275911*math.sqrt(0.5))*ax)
    e=jnp.exp2((-0.5/math.log(2.0))*(x*x))
    p=0.5*0.254829592+t*(0.5*-0.284496736+t*(0.5*1.421413741+t*(0.5*-1.453152027+t*(0.5*1.061405429))))
    return jnp.maximum(x,0.0)-ax*(p*t*e)

def norm(v,g):
    c=v-jnp.mean(v,-1,keepdims=True)
    var=jnp.mean(c*c,-1,keepdims=True)
    return c*lax.rsqrt(var+1e-5)*g

ORDER = ((2, 1), (2, 0), (1, 1), (3, 1), (1, 0), (3, 0), (0, 1), (0, 0))
UNITS = ((0, 0), (0, 1), (0, 2), (1, 0), (2, 0), (3, 0))
ROWS = (128, 64, 128, 256)


PLAN = {
    2: ((0, 0), (1, 0)),
    3: ((0, 1), (2, 0)),
    4: ((1, 1), (3, 0)),
    5: ((0, 2), (2, 1)),
    6: ((1, 2), (3, 1)),
    7: ((2, 2), (4, 0)),
}


def inverse(k):
    return ((4 - k // 4) % 4) * 4 + k % 4


def whole_kernel(
    own,
    pay,
    qry,
    psg_in,
    wq_i,
    wo_i,
    wu_i,
    wd_i,
    g1,
    g2,
    out,
    wq,
    wo,
    wu,
    wd,
    tok,
    psg_qk,
    reply_vc,
    kl,
    vl,
    ctxl,
    acc,
    ask,
    asked,
    msg,
    got,
    hot,
    back,
    codes,
    score,
    pool,
    prow,
    flatcol,
    psem,
    qsem,
    msem,
    rsem,
    osem,
    wsend,
    wrecv,
    lsem,
    fsem,
):
    psg, qs, ks, vs, ctx = (
        psg_qk.at[:PASS_DEV],
        psg_qk.at[:N_TOK],
        psg_qk.at[N_TOK:],
        reply_vc.at[:N_TOK],
        reply_vc.at[N_TOK:],
    )
    idx = lax.axis_index("index")
    z = lax.axis_index("rep")
    t = lax.axis_index("tp")
    y, xh, c = idx // 4, (idx // 2) % 2, idx % 2

    def peer(k):
        dy, dx, dc = k // 4, (k // 2) % 2, k % 2
        return (((y + dy) % 4) * 4 + ((xh + dx) % 2) * 2 + (c + dc) % 2, z, (t + dx) % 2)

    partner = (idx, z, 1 - t)
    z_up = (idx, (z + 1) % 4, t)
    z_down = (idx, (z + 3) % 4, t)
    barrier = pltpu.get_barrier_semaphore()
    for device in [peer(k) for k in range(1, 16)] + [partner, z_up, z_down]:
        pl.semaphore_signal(barrier, inc=1, device_id=device, device_id_type=MESH)
    load = pltpu.make_async_copy(psg_in, psg, psem)
    load.start()

    owner = own[...]
    rel = (((owner >> 2) - y) & 3) * 4 + (((owner >> 1) & 1) ^ xh) * 2 + ((owner & 1) ^ c)
    rel = jnp.where(owner < 0, -1, rel).astype(f32)
    sub16 = lax.broadcasted_iota(jnp.int32, (16, 128), 0).astype(f32)
    marks = [jnp.where(rel[r : r + 1, :] == sub16, 1.0, 0.0) for r in range(16)]
    onehot = jnp.concatenate(marks, 0)
    onehot16 = onehot.astype(bf16)
    row128 = lax.broadcasted_iota(jnp.int32, (128, 128), 0)
    col128 = lax.broadcasted_iota(jnp.int32, (128, 128), 1)
    same = (row128 // 64) == (col128 // 64)
    earlier = jnp.where(same & (row128 < col128), 1.0, 0.0).astype(bf16)
    block = jnp.where(same, 1.0, 0.0).astype(bf16)
    row256 = lax.broadcasted_iota(jnp.int32, (256, 256), 0)
    col256 = lax.broadcasted_iota(jnp.int32, (256, 256), 1)
    above = jnp.where(((row256 % 16) == (col256 % 16)) & (col256 < row256 - row256 % 16), 1.0, 0.0)
    lists_before = jnp.dot(above.astype(bf16), onehot16, preferred_element_type=f32).astype(bf16)
    count = jnp.dot(onehot16, earlier, preferred_element_type=f32)
    count = count + jnp.dot(lists_before, block, preferred_element_type=f32)
    slot = jnp.sum((onehot * count).reshape(16, 16, 128), 1)

    lane16 = lax.broadcasted_iota(jnp.int32, (16, 128), 1)
    target = jnp.where(lane16 < 64, slot, slot + 128.0)
    high = (pay[...] >> 5).astype(f32)
    low = (pay[...] & 31).astype(f32)
    sub256 = lax.broadcasted_iota(jnp.int32, (256, 128), 0).astype(f32)
    pad = jnp.zeros((96, 128), f32)
    table = jnp.zeros((256, 128), f32)
    for r in range(16):
        here = jnp.where(target[r : r + 1, :] == sub256, 1.0, 0.0).astype(bf16)
        digit = jnp.concatenate([marks[r] * high[r : r + 1, :], marks[r] * low[r : r + 1, :], pad], 0)
        table = table + lax.dot_general(here, digit.astype(bf16), NT, preferred_element_type=f32)
    table = jnp.transpose(table)
    table = table[:16] * 32.0 + table[16:32]
    first_row = lax.broadcasted_iota(jnp.int32, (8, 128), 0) == 0
    for k in range(16):
        msg[k] = jnp.where(first_row, table[k : k + 1, :128], table[k : k + 1, 128:])
    got[0] = msg[0]

    wide = lax.broadcasted_iota(jnp.int32, (16, 128), 1).astype(f32)
    mix = jnp.zeros((16, 128), f32)
    for j in range(4):
        place = rel[:, 64 + j : 65 + j] * 8.0 + slot[:, 64 + j : 65 + j]
        mix = mix + jnp.where(place == wide, 1.0, 0.0)
    pick = jnp.transpose(jnp.concatenate([mix, jnp.zeros((112, 128), f32)], 0)).astype(bf16)
    padded = jnp.concatenate([qry[...], jnp.zeros((112, D), bf16)], 0)
    picked = jnp.dot(pick, padded, preferred_element_type=f32)

    def fold(rows):
        return jnp.concatenate([rows[:, :512], rows[:, 512:]], 0).astype(bf16)

    for k in range(16):
        ask[k] = fold(picked[k * 8 : (k + 1) * 8])
    asked[0] = ask[0]

    pl.semaphore_wait(barrier, 18)

    def remote(src, dst, sems, k):
        copy = pltpu.make_async_remote_copy(
            src_ref=src,
            dst_ref=dst,
            send_sem=sems.at[0, k],
            recv_sem=sems.at[1, inverse(k)],
            device_id=peer(k),
            device_id_type=MESH,
        )
        copy.start()
        return copy

    steps = [dy * 4 + dx * 2 for dy, dx in ORDER]
    pairs = [k for first in steps for k in (first, first + 1) if k]
    m_copy = {k: remote(msg.at[k], got.at[inverse(k)], msem, k) for k in pairs}
    q_copy = {k: remote(ask.at[k], asked.at[inverse(k)], qsem, k) for k in pairs}

    w_in = (wq_i, wo_i, wu_i, wd_i)
    w_out = (wq.at[1], wo.at[1], wu.at[1], wd.at[1])

    def share(refs, unit, zz, cc, half=None):
        n, j = UNITS[unit]
        rows = ROWS[n]
        start = (zz * 2 + cc) * rows
        if half is not None:
            rows = rows // 2
            start = start + half * rows
        part = pl.ds(pl.multiple_of(start, 32), rows)
        return refs[n].at[j, part, :] if n == 0 else refs[n].at[part, :]

    def push(src, dst, unit, s, device):
        copy = pltpu.make_async_remote_copy(
            src_ref=src,
            dst_ref=dst,
            send_sem=wsend.at[unit, s],
            recv_sem=wrecv.at[unit, s],
            device_id=device,
            device_id_type=MESH,
        )
        copy.start()
        return copy

    started = {}
    for u in range(6):
        started[u, 0] = push(share(w_in, u, z, c), share(w_out, u, z, c), u, 0, partner)
    own_copies = []
    for n, here in enumerate((wq, wo, wu, wd)):
        own_copies.append(pltpu.make_async_copy(w_in[n], here.at[0], lsem.at[n]))
        own_copies[n].start()

    def relay(u, stage):
        def put(s, zz, half, device):
            ref = share(w_out, u, zz, c, half)
            started[u, s] = push(ref, ref, u, s, device)

        zm, zp, zo = (z + 3) % 4, (z + 1) % 4, (z + 2) % 4
        if stage == 0:
            started[u, 0].wait_recv()
            put(1, z, None, z_up)
            put(2, z, None, z_down)
            put(5, z, None, peer(1))
        elif stage == 1:
            started[u, 1].wait_recv()
            put(3, zm, 0, z_up)
            put(6, zm, None, peer(1))
            started[u, 2].wait_recv()
            put(4, zp, 1, z_down)
            put(7, zp, None, peer(1))
        else:
            started[u, 3].wait_recv()
            started[u, 4].wait_recv()
            put(8, zo, None, peer(1))

    def landed(*units):
        for u in units:
            for s in range(5, 9):
                started[u, s].wait_recv()

    flat = rel * 128.0 + slot
    eye = row128 == col128
    for r in range(16):
        column = jnp.sum(jnp.where(eye[:64], flat[r : r + 1, :], 0.0), 1, keepdims=True)
        flatcol[r * 64 : (r + 1) * 64, :] = jnp.broadcast_to(column, (64, 128))

    def probes():
        eye8 = eye[:8]
        for k in range(16):
            column = jnp.sum(jnp.where(eye8, got[k, 1:2, :], 0.0), 1, keepdims=True)
            codes[k * 8 : (k + 1) * 8, :] = jnp.broadcast_to(column, (8, 128))
        for k in pairs:
            q_copy[k].wait_recv()
        cluster = codes[:, 0:1].astype(jnp.int32) & 3
        rows16 = asked[...].reshape(256, 512)

        def score_step(n, carry):
            rows = pl.ds(pl.multiple_of(n * 512, 512), 512)
            left = lax.dot_general(rows16, psg[rows, :512], NT, preferred_element_type=f32)
            right = lax.dot_general(rows16, psg[rows, 512:], NT, preferred_element_type=f32)
            s = left.reshape(16, 2, 8, 512)[:, 0] + right.reshape(16, 2, 8, 512)[:, 1]
            score[:, rows] = jnp.where(cluster == n, s.reshape(128, 512) * (D ** (-0.5)), -1e30)
            return carry

        lax.fori_loop(0, 4, score_step, 0)
        peak = jnp.max(score[...], 1, keepdims=True)
        expo = jnp.exp(score[...] - peak)
        weights = (expo / jnp.sum(expo, 1, keepdims=True)).astype(bf16)
        pooled = jnp.dot(weights, psg[...], preferred_element_type=f32)
        for k in range(16):
            rows = fold(pooled[k * 8 : (k + 1) * 8])
            if k:
                pool[k] = rows
            else:
                prow[0] = rows
        return {k: remote(pool.at[k], prow.at[inverse(k)], osem, k) for k in pairs}

    load.wait()
    r_copy = {}
    waited = set()
    lanes = lax.broadcasted_iota(jnp.int32, (128, 2048), 1).astype(f32)
    for number, first in enumerate(steps):
        for k in (first, first + 1):
            if k and k not in waited:
                m_copy[inverse(k)].wait_recv()
                waited.add(k)
            column = jnp.sum(jnp.where(eye, got[k, 0:1, :], 0.0), 1, keepdims=True)
            hot[(k % 2) * 128 : (k % 2 + 1) * 128, :] = jnp.where(column == lanes, 1.0, 0.0).astype(bf16)

        def gather(n, carry, first=first):
            cols = pl.ds(pl.multiple_of(n * 256, 256), 256)
            rows = jnp.dot(hot[...], psg[:, cols], preferred_element_type=f32).astype(bf16)
            if first:
                reply_vc[first * 128 : (first + 1) * 128, cols] = rows[:128]
            else:
                back[0, :, cols] = rows[:128]
            reply_vc[(first + 1) * 128 : (first + 2) * 128, cols] = rows[128:]
            return carry

        lax.fori_loop(0, 4, gather, 0)
        for k in (first, first + 1):
            if k:
                r_copy[k] = remote(reply_vc.at[k * 128 : (k + 1) * 128], back.at[inverse(k)], rsem, k)
        if number == 2:
            for k in pairs:
                if k not in waited:
                    m_copy[inverse(k)].wait_recv()
                    waited.add(k)
            p_copy = probes()
        for u, stage in PLAN.get(number, ()):
            relay(u, stage)

    def assemble(dy, fresh):
        for k in range(dy * 4, dy * 4 + 4):
            if k:
                r_copy[inverse(k)].wait_recv()
        wide = (lax.broadcasted_iota(jnp.int32, (256, 512), 1) + dy * 512).astype(f32)

        def part(n, carry):
            rows = pl.ds(pl.multiple_of(n * 256, 256), 256)
            place = jnp.concatenate([flatcol[rows, :]] * 4, 1)
            mark = jnp.where(place == wide, 1.0, 0.0).astype(bf16)
            values = back[dy * 4 : dy * 4 + 4].reshape(512, D)
            found = jnp.dot(mark, values, preferred_element_type=f32).astype(bf16)
            tok[rows, :] = found if fresh else tok[rows, :] + found
            return carry

        lax.fori_loop(0, 4, part, 0)

    relay(3, 2)
    assemble(0, True)
    relay(4, 1)
    assemble(2, False)
    relay(5, 0)
    for k in pairs:
        p_copy[k].wait_recv()
    wide = lax.broadcasted_iota(jnp.int32, (16, 256), 1).astype(f32)
    halves = []
    for half in range(2):
        mix = jnp.zeros((16, 256), f32)
        for j in range(4):
            place = rel[:, 64 + j : 65 + j] * 16.0 + slot[:, 64 + j : 65 + j] + half * 8.0
            mix = mix + jnp.where(place == wide, 1.0, 0.0)
        halves.append(
            jnp.dot(mix.astype(bf16), prow[...].reshape(256, 512), preferred_element_type=f32)
        )
    summed = jnp.concatenate(halves, 1)
    tok[N_C:, :] = (qry[...].astype(f32) + summed * 0.25).astype(bf16)
    assemble(1, False)
    assemble(3, False)
    for copy in r_copy.values():
        copy.wait_send()

    for i in range(2):
        if i == 0:
            own_copies[0].wait()
        else:
            landed(0, 1, 2)
        def qkv_step(n,carry):
            col=pl.ds(pl.multiple_of(n*256,256),256)
            ocol=pl.ds(pl.multiple_of(i*512+n*256,256),256)
            for j,ref in enumerate((qs,ks,vs)):
                r=jnp.dot(tok[...],wq[i,j,:,col],preferred_element_type=f32)
                if j==0: r=r*0.125
                ref[:,ocol]=r.astype(bf16)
            return carry
        lax.fori_loop(0,2,qkv_step,0)
    relay(4, 2)
    relay(5, 1)
    kl[...]=ks[N_C:,:].astype(f32); vl[...]=vs[N_C:,:].astype(f32)
    ctxl[...]=jnp.zeros_like(ctxl)
    lane=lax.broadcasted_iota(jnp.int32,(64,256),1)//64
    ones_bd=(lax.broadcasted_iota(jnp.int32,(256,256),0)//64==lax.broadcasted_iota(jnp.int32,(256,256),1)//64).astype(bf16)
    low=lax.broadcasted_iota(jnp.int32,(80,128),1)<64
    rowid=lax.broadcasted_iota(jnp.int32,(16,256),0)
    def bd(x):
        return jnp.concatenate([jnp.where(lane==h,x,jnp.zeros_like(x)) for h in range(4)],0)
    def att(g,carry):
        rows=pl.ds(pl.multiple_of(g*64,64),64)
        es=[];els=[];
        for j in range(4):
            cs=slice(j*256,(j+1)*256)
            Q=jnp.concatenate([qs[rows,cs],qs[N_C:,cs]],0)
            klb=jnp.broadcast_to(kl[pl.ds(g,1),cs],(64,256)).astype(bf16)
            S=lax.dot_general(Q,bd(ks[rows,cs]),NT,preferred_element_type=f32)
            SL=lax.dot_general(Q,bd(klb),NT,preferred_element_type=f32)
            ms=[]
            for b in range(2):
                X=S[:,b*128:(b+1)*128]
                mA=jnp.max(jnp.where(low,X,-jnp.inf),1,keepdims=True)
                mB=jnp.max(jnp.where(low,-jnp.inf,X),1,keepdims=True)
                ms.append(jnp.where(low,mA,mB))
            m=jnp.maximum(jnp.concatenate(ms,1),SL)
            es.append(jnp.exp(S-m).astype(bf16)); els.append(jnp.exp(SL-m))
        den=jnp.dot(jnp.concatenate(es,0),ones_bd,preferred_element_type=f32)
        for j in range(4):
            cs=slice(j*256,(j+1)*256)
            pv=jnp.dot(es[j],bd(vs[rows,cs]),preferred_element_type=f32)
            c=(pv+els[j]*vl[pl.ds(g,1),cs])/(den[j*80:(j+1)*80]+els[j])
            ctx[rows,cs]=c[:64].astype(bf16)
            ctxl[:,cs]+=jnp.where(rowid==g,c[64:],0.0)
        return carry
    lax.fori_loop(0,16,att,0)
    ctx[N_C:,:]=ctxl[...].astype(bf16)
    relay(5, 2)
    own_copies[1].wait()
    landed(3)
    def outp(rows,n):
        a=jnp.dot(ctx[rows,:512],wo[0],preferred_element_type=f32)+jnp.dot(ctx[rows,512:],wo[1],preferred_element_type=f32)
        return norm(tok[rows,:].astype(f32)+a,g1[...]).astype(bf16).astype(f32)
    def put(g,y):
        for c in range(8): acc[c,pl.ds(16+g,64,stride=16),:]=y[:,c*128:(c+1)*128]
    def outc(i,carry):
        h=outp(pl.ds(pl.multiple_of(i*256,256),256),256)
        for l in range(4):
            put(i*4+l,h[l*64:(l+1)*64])
        return carry
    lax.fori_loop(0,3,outc,0)
    h=outp(slice(768,1040),272)
    for l in range(4):
        put(12+l,h[l*64:(l+1)*64])
    for c in range(8): acc[c,0:16,:]=h[256:,c*128:(c+1)*128]
    own_copies[2].wait()
    own_copies[3].wait()
    landed(4, 5)
    def ffn(r,carry):
        rows=pl.ds(pl.multiple_of(r*208,16),208)
        t=jnp.concatenate([acc[c,rows,:] for c in range(8)],1)
        x=t.astype(bf16)
        acts=[]
        for i in range(2):
            for n in range(4):
                u=jnp.dot(x,wu[i,:,n*512:(n+1)*512],preferred_element_type=f32)
                acts.append(gelu(u).astype(bf16))
        for i in range(2):
            t=t+jnp.dot(jnp.concatenate(acts[i*4:(i+1)*4],1),wd[i],preferred_element_type=f32)
        tok[rows,:]=norm(t,g2[...]).astype(bf16)
        pltpu.make_async_copy(tok.at[rows],out.at[rows],fsem.at[r]).start()
        return carry
    lax.fori_loop(0,5,ffn,0)
    for r in range(5):
        rows=slice(r*208,(r+1)*208)
        pltpu.make_async_copy(tok.at[rows],out.at[rows],fsem.at[r]).wait()
    for copies in (m_copy, q_copy, p_copy, started):
        for copy in copies.values():
            copy.wait_send()


def whole(own, pay, qry, passages, wq, wo, wu, wd, g1, g2):
    vmem = pl.BlockSpec(memory_space=pltpu.VMEM)
    hbm = pl.BlockSpec(memory_space=pl.ANY)
    dma = pltpu.SemaphoreType.DMA
    return pl.pallas_call(
        whole_kernel,
        out_shape=jax.ShapeDtypeStruct((N_TOK, D), bf16),
        in_specs=[vmem, vmem, vmem] + [hbm] * 5 + [vmem, vmem],
        out_specs=hbm,
        scratch_shapes=[
            pltpu.VMEM((2, 3, D, 512), bf16),
            pltpu.VMEM((2, 512, D), bf16),
            pltpu.VMEM((2, D, 2048), bf16),
            pltpu.VMEM((2, 2048, D), bf16),
            pltpu.VMEM((N_TOK, D), bf16),
            pltpu.VMEM((2 * N_TOK, D), bf16),
            pltpu.VMEM((2 * N_TOK, D), bf16),
            pltpu.VMEM((16, D), f32),
            pltpu.VMEM((16, D), f32),
            pltpu.VMEM((16, D), f32),
            pltpu.VMEM((8, N_TOK, 128), f32),
            pltpu.VMEM((16, 16, 512), bf16),
            pltpu.VMEM((16, 16, 512), bf16),
            pltpu.VMEM((16, 8, 128), f32),
            pltpu.VMEM((16, 8, 128), f32),
            pltpu.VMEM((256, 2048), bf16),
            pltpu.VMEM((16, 128, D), bf16),
            pltpu.VMEM((128, 128), f32),
            pltpu.VMEM((128, PASS_DEV), f32),
            pltpu.VMEM((16, 16, 512), bf16),
            pltpu.VMEM((16, 16, 512), bf16),
            pltpu.VMEM((N_C, 128), f32),
            dma(()),
            dma((2, 16)),
            dma((2, 16)),
            dma((2, 16)),
            dma((2, 16)),
            dma((6, 9)),
            dma((6, 9)),
            dma((4,)),
            dma((5,)),
        ],
        compiler_params=pltpu.CompilerParams(
            collective_id=0, has_side_effects=True, vmem_limit_bytes=62 * 2**20
        ),
        cost_estimate=pl.CostEstimate(flops=2**35, bytes_accessed=50 * 2**20, transcendentals=0),
        name="whole",
    )(own, pay, qry, passages, wq, wo, wu, wd, g1, g2)


def on_device(
    queries,
    passages,
    probe_owner,
    probe_cluster,
    pair_owner,
    pair_row,
    w_qkv,
    w_out,
    w_up,
    w_down,
    gain_one,
    gain_two,
):
    blank = jnp.full((Q_DEV, 60), -1, jnp.int32)
    own = jnp.concatenate([pair_owner[:, :, 0], probe_owner, blank], 1)
    pay = jnp.concatenate([pair_row, probe_cluster, blank * 0], 1)
    wq = jnp.transpose(w_qkv, (1, 0, 2))
    rows = whole(
        own, pay, queries, passages, wq, w_out, w_up, w_down, gain_one[None, :], gain_two[None, :]
    )
    return jnp.transpose(rows.reshape(65, 16, D), (1, 0, 2))


def solution(mesh):
    rows = P(("index", "rep", "tp"), None)
    lists = P(("index", "rep", "tp"), None, None)
    in_specs = (
        rows,
        P("index", None),
        rows,
        rows,
        lists,
        rows,
        P(None, None, "tp"),
        P("tp", None),
        P(None, "tp"),
        P("tp", None),
        P(),
        P(),
    )
    return jax.shard_map(
        on_device, mesh=mesh, in_specs=in_specs, out_specs=lists, check_vma=False
    )
```

time: 156 us -> 139 us (0.89)
  Pallas kernels: 152 us -> 132 us
  local copies, waits for them, and re-layouts: 1.67 us -> 4.92 us
    pallas_call x2 -> x1, Pallas kernels: 152 us -> 132 us  [whole(): pl.pallas_call(whole_kernel, out_shape=jax.ShapeDtypeStruct((N_TOK, D), b...]
    unnamed x2 -> x3, local copies, waits for them, and re-layouts: 1.51 us -> 4.76 us
where the time goes in v2:
time: 139 us
  Pallas kernels  132 us (95%)
  local copies, waits for them, and re-layouts  4.92 us (4%)
    pallas_call x1, Pallas kernels, whole(): pl.pallas_call(whole_kernel, out_shape=jax.ShapeDtypeStruct((N_TOK, D), b...  132 us
    unnamed x3, local copies, waits for them, and re-layouts  4.76 us

profile of v2, /device:TPU:1, one launch (start us, length us, event | category | flops | bytes accessed | tf_op | source)
XLA Modules:
  0.0 138.7 jit_solution(57762218674522824)
XLA Ops:
  0.0 0.1 pad.5.clone
  0.1 0.1 pad.2.clone
  0.2 0.8 copy.13
  0.9 0.8 copy.14
  1.7 1.4 %add_add_fusion = (s32[16,128]{1,0:T(8,128)}, s32[16,128]{1,0:T(8,128)}) fusion(s32[16,4]{1,0:T(8,128)S(1)} %copy.13, s32[16,64]{1,0:T(8,128)} %bitcast.8, s32[128]{0:T(128)S(1)} %pad.5.clone, s32[128]{0:T(128)S(1)} %pad.2.clone, s32[16,4]{1,0:T(8,128)S(1)} %copy.14, s32[16,64]{1,0:T(8,128)} %param.17), kind=kLoop, calls=%fused_computation | loop fusion | flops 8192 | bytes 26112 | tf_op jit(solution)/shard_map/concatenate | solution.py:527
  3.1 132.4 %whole.1 = bf16[1040,1024]{1,0:T(8,128)(2,1)} custom-call(s32[16,128]{1,0:T(8,128)} %get-tuple-element.5.own, s32[16,128]{1,0:T(8,128)} %get-tuple-element.6.pay, bf16[16,1024]{1,0:T(8,128)(2,1)} %qry.1, bf16[2048,1024]{1,0:T(8,128)(2,1)} %psg_in.1, bf16[3,1024,512]{2,1,0:T(8,128)(2,1)} %bitcast.9, bf16[512,1024]{1,0:T(8,128)(2,1)} %wo_i.1, ...), custom_call_target="tpu_custom_call" | custom-call | flops 34359738368 | bytes 52428800 | tf_op jit(solution)/shard_map/whole/pallas_call | solution.py:466
  135.5 3.2 %copy.16 = bf16[16,65,1024]{2,0,1:T(8,128)(2,1)} copy(bf16[16,65,1024]{2,0,1:T(8,128)(2,1)} %bitcast.7) | data formatting | bytes 4259840
  (2 shorter events, 0.0 us)

commit v3 on v2

--- a/solution.py
+++ b/solution.py
@@ -67,7 +67,7 @@
     tok,
     psg_qk,
     reply_vc,
-    kl,
+    sl,
     vl,
     ctxl,
     acc,
@@ -111,8 +111,9 @@
     partner = (idx, z, 1 - t)
     z_up = (idx, (z + 1) % 4, t)
     z_down = (idx, (z + 3) % 4, t)
+    z_across = (idx, (z + 2) % 4, t)
     barrier = pltpu.get_barrier_semaphore()
-    for device in [peer(k) for k in range(1, 16)] + [partner, z_up, z_down]:
+    for device in [peer(k) for k in range(1, 16)] + [partner, z_up, z_down, z_across]:
         pl.semaphore_signal(barrier, inc=1, device_id=device, device_id_type=MESH)
     load = pltpu.make_async_copy(psg_in, psg, psem)
     load.start()
@@ -171,7 +172,7 @@
         ask[k] = fold(picked[k * 8 : (k + 1) * 8])
     asked[0] = ask[0]
 
-    pl.semaphore_wait(barrier, 18)
+    pl.semaphore_wait(barrier, 19)
 
     def remote(src, dst, sems, k):
         copy = pltpu.make_async_remote_copy(
@@ -233,7 +234,13 @@
             started[u, 0].wait_recv()
             put(1, z, None, z_up)
             put(2, z, None, z_down)
+            if u >= 4:
+                put(3, z, None, z_across)
             put(5, z, None, peer(1))
+        elif u >= 4:
+            for s, zz in ((1, zm), (2, zp), (3, zo)):
+                started[u, s].wait_recv()
+                put(s + 5, zz, None, peer(1))
         elif stage == 1:
             started[u, 1].wait_recv()
             put(3, zm, 0, z_up)
@@ -342,7 +349,6 @@
 
     relay(3, 2)
     assemble(0, True)
-    relay(4, 1)
     assemble(2, False)
     relay(5, 0)
     for k in pairs:
@@ -379,24 +385,40 @@
             return carry
         lax.fori_loop(0,2,qkv_step,0)
     relay(4, 2)
-    relay(5, 1)
-    kl[...]=ks[N_C:,:].astype(f32); vl[...]=vs[N_C:,:].astype(f32)
+    vl[...]=vs[N_C:,:].astype(f32)
     ctxl[...]=jnp.zeros_like(ctxl)
     lane=lax.broadcasted_iota(jnp.int32,(64,256),1)//64
     ones_bd=(lax.broadcasted_iota(jnp.int32,(256,256),0)//64==lax.broadcasted_iota(jnp.int32,(256,256),1)//64).astype(bf16)
+    bd_mask=lax.broadcasted_iota(jnp.int32,(256,256),0)//64==lax.broadcasted_iota(jnp.int32,(256,256),1)//64
     low=lax.broadcasted_iota(jnp.int32,(80,128),1)<64
     rowid=lax.broadcasted_iota(jnp.int32,(16,256),0)
     def bd(x):
         return jnp.concatenate([jnp.where(lane==h,x,jnp.zeros_like(x)) for h in range(4)],0)
+    lead_mask=lax.broadcasted_iota(jnp.int32,(16,256),1)//64
+    for j in range(4):
+        cs=slice(j*256,(j+1)*256)
+        kj=ks[N_C:,cs]
+        rows_hl=jnp.concatenate([jnp.where(lead_mask==h,kj,jnp.zeros_like(kj)) for h in range(4)]+[jnp.zeros((64,256),bf16)],0)
+        sl[:,j*128:(j+1)*128]=lax.dot_general(qs[:,cs],rows_hl,NT,preferred_element_type=f32)
+    erow=lax.broadcasted_iota(jnp.int32,(256,256),0)%128
+    ecol=lax.broadcasted_iota(jnp.int32,(256,256),1)
     def att(g,carry):
         rows=pl.ds(pl.multiple_of(g*64,64),64)
-        es=[];els=[];
+        expand=jnp.where(erow==(ecol//64)*16+g,1.0,0.0).astype(bf16)
+        parts=[]
+        for j in range(4):
+            x=jnp.concatenate([sl[rows,j*128:(j+1)*128],sl[N_C:,j*128:(j+1)*128]],0)
+            hi=x.astype(bf16)
+            parts.append(jnp.concatenate([hi,(x-hi.astype(f32)).astype(bf16)],1))
+        SLall=jnp.dot(jnp.concatenate(parts,0),expand,preferred_element_type=f32)
+        es=[];els=[]
         for j in range(4):
             cs=slice(j*256,(j+1)*256)
             Q=jnp.concatenate([qs[rows,cs],qs[N_C:,cs]],0)
-            klb=jnp.broadcast_to(kl[pl.ds(g,1),cs],(64,256)).astype(bf16)
-            S=lax.dot_general(Q,bd(ks[rows,cs]),NT,preferred_element_type=f32)
-            SL=lax.dot_general(Q,bd(klb),NT,preferred_element_type=f32)
+            kt=jnp.transpose(jnp.concatenate([ks[rows,cs],ks[rows,cs]],0))
+            kt=jnp.concatenate([kt,kt],1)
+            S=jnp.dot(Q,jnp.where(bd_mask,kt,jnp.zeros_like(kt)),preferred_element_type=f32)
+            SL=SLall[j*80:(j+1)*80]
             ms=[]
             for b in range(2):
                 X=S[:,b*128:(b+1)*128]
@@ -413,7 +435,7 @@
             ctx[rows,cs]=c[:64].astype(bf16)
             ctxl[:,cs]+=jnp.where(rowid==g,c[64:],0.0)
         return carry
-    lax.fori_loop(0,16,att,0)
+    lax.fori_loop(0, 16, att, 0, unroll=4)
     ctx[N_C:,:]=ctxl[...].astype(bf16)
     relay(5, 2)
     own_copies[1].wait()
@@ -476,7 +498,7 @@
             pltpu.VMEM((N_TOK, D), bf16),
             pltpu.VMEM((2 * N_TOK, D), bf16),
             pltpu.VMEM((2 * N_TOK, D), bf16),
-            pltpu.VMEM((16, D), f32),
+            pltpu.VMEM((N_TOK, 512), f32),
             pltpu.VMEM((16, D), f32),
             pltpu.VMEM((16, D), f32),
             pltpu.VMEM((8, N_TOK, 128), f32),

time: 139 us -> 135 us (0.971)
  Pallas kernels: 132 us -> 128 us
    pallas_call x1, Pallas kernels: 132 us -> 128 us  [whole(): pl.pallas_call(whole_kernel, out_shape=jax.ShapeDtypeStruct((N_TOK, D), b...]
where the time goes in v3:
time: 135 us; the launch traced here: 134 us
  Pallas kernels  128 us (95%)
  local copies, waits for them, and re-layouts  4.92 us (4%)
  other arithmetic  1.39 us (1%)
    pallas_call x1, Pallas kernels, whole(): pl.pallas_call(whole_kernel, out_shape=jax.ShapeDtypeStruct((N_TOK, D), b...  128 us
    unnamed x3, local copies, waits for them, and re-layouts  4.76 us

profile of v3, /device:TPU:1, one launch (start us, length us, event | category | flops | bytes accessed | tf_op | source)
XLA Modules:
  0.0 134.2 jit_solution(2553316005699437641)
XLA Ops:
  0.0 0.1 pad.5.clone
  0.1 0.1 pad.2.clone
  0.2 0.8 copy.13
  0.9 0.8 copy.14
  1.7 1.4 %add_add_fusion = (s32[16,128]{1,0:T(8,128)}, s32[16,128]{1,0:T(8,128)}) fusion(s32[16,4]{1,0:T(8,128)S(1)} %copy.13, s32[16,64]{1,0:T(8,128)} %bitcast.8, s32[128]{0:T(128)S(1)} %pad.5.clone, s32[128]{0:T(128)S(1)} %pad.2.clone, s32[16,4]{1,0:T(8,128)S(1)} %copy.14, s32[16,64]{1,0:T(8,128)} %param.17), kind=kLoop, calls=%fused_computation | loop fusion | flops 8192 | bytes 26112 | tf_op jit(solution)/shard_map/concatenate | solution.py:549
  3.1 127.9 %whole.1 = bf16[1040,1024]{1,0:T(8,128)(2,1)} custom-call(s32[16,128]{1,0:T(8,128)} %get-tuple-element.5.own, s32[16,128]{1,0:T(8,128)} %get-tuple-element.6.pay, bf16[16,1024]{1,0:T(8,128)(2,1)} %qry.1, bf16[2048,1024]{1,0:T(8,128)(2,1)} %psg_in.1, bf16[3,1024,512]{2,1,0:T(8,128)(2,1)} %bitcast.9, bf16[512,1024]{1,0:T(8,128)(2,1)} %wo_i.1, ...), custom_call_target="tpu_custom_call" | custom-call | flops 34359738368 | bytes 52428800 | tf_op jit(solution)/shard_map/whole/pallas_call | solution.py:488
  131.0 3.2 %copy.16 = bf16[16,65,1024]{2,0,1:T(8,128)(2,1)} copy(bf16[16,65,1024]{2,0,1:T(8,128)(2,1)} %bitcast.7) | data formatting | bytes 4259840
  (2 shorter events, 0.0 us)

commit v4 on v3

--- a/solution.py
+++ b/solution.py
@@ -49,8 +49,10 @@
 
 
 def whole_kernel(
-    own,
-    pay,
+    p_own,
+    p_row,
+    o_own,
+    o_clu,
     qry,
     psg_in,
     wq_i,
@@ -91,6 +93,9 @@
     wrecv,
     lsem,
     fsem,
+    flip,
+    wide_own,
+    wide_row,
 ):
     psg, qs, ks, vs, ctx = (
         psg_qk.at[:PASS_DEV],
@@ -118,7 +123,18 @@
     load = pltpu.make_async_copy(psg_in, psg, psem)
     load.start()
 
-    owner = own[...]
+    flip[...] = jnp.zeros_like(flip)
+    flip[0, 64:68, 0:16] = o_own[...].astype(f32)
+    flip[1, 64:68, 0:16] = o_clu[...].astype(f32)
+    wide_own[...] = jnp.zeros_like(wide_own)
+    wide_row[...] = jnp.zeros_like(wide_row)
+    for r in range(16):
+        wide_own[r : r + 1, 0:64] = p_own[r]
+    wide_row[:, 0:64] = p_row[...]
+    lane16 = lax.broadcasted_iota(jnp.int32, (16, 128), 1)
+    owner = wide_own[...] + jnp.transpose(flip[0])[:16].astype(jnp.int32)
+    owner = jnp.where(lane16 < 68, owner, -1)
+    payload = wide_row[...] + jnp.transpose(flip[1])[:16].astype(jnp.int32)
     rel = (((owner >> 2) - y) & 3) * 4 + (((owner >> 1) & 1) ^ xh) * 2 + ((owner & 1) ^ c)
     rel = jnp.where(owner < 0, -1, rel).astype(f32)
     sub16 = lax.broadcasted_iota(jnp.int32, (16, 128), 0).astype(f32)
@@ -138,10 +154,9 @@
     count = count + jnp.dot(lists_before, block, preferred_element_type=f32)
     slot = jnp.sum((onehot * count).reshape(16, 16, 128), 1)
 
-    lane16 = lax.broadcasted_iota(jnp.int32, (16, 128), 1)
     target = jnp.where(lane16 < 64, slot, slot + 128.0)
-    high = (pay[...] >> 5).astype(f32)
-    low = (pay[...] & 31).astype(f32)
+    high = (payload >> 5).astype(f32)
+    low = (payload & 31).astype(f32)
     sub256 = lax.broadcasted_iota(jnp.int32, (256, 128), 0).astype(f32)
     pad = jnp.zeros((96, 128), f32)
     table = jnp.zeros((256, 128), f32)
@@ -348,8 +363,7 @@
         lax.fori_loop(0, 4, part, 0)
 
     relay(3, 2)
-    assemble(0, True)
-    assemble(2, False)
+    assemble(2, True)
     relay(5, 0)
     for k in pairs:
         p_copy[k].wait_recv()
@@ -367,6 +381,7 @@
     tok[N_C:, :] = (qry[...].astype(f32) + summed * 0.25).astype(bf16)
     assemble(1, False)
     assemble(3, False)
+    assemble(0, False)
     for copy in r_copy.values():
         copy.wait_send()
 
@@ -481,14 +496,14 @@
             copy.wait_send()
 
 
-def whole(own, pay, qry, passages, wq, wo, wu, wd, g1, g2):
+def whole(p_own, p_row, o_own, o_clu, qry, passages, wq, wo, wu, wd, g1, g2):
     vmem = pl.BlockSpec(memory_space=pltpu.VMEM)
     hbm = pl.BlockSpec(memory_space=pl.ANY)
     dma = pltpu.SemaphoreType.DMA
     return pl.pallas_call(
         whole_kernel,
         out_shape=jax.ShapeDtypeStruct((N_TOK, D), bf16),
-        in_specs=[vmem, vmem, vmem] + [hbm] * 5 + [vmem, vmem],
+        in_specs=[vmem] * 5 + [hbm] * 5 + [vmem, vmem],
         out_specs=hbm,
         scratch_shapes=[
             pltpu.VMEM((2, 3, D, 512), bf16),
@@ -522,13 +537,16 @@
             dma((6, 9)),
             dma((4,)),
             dma((5,)),
+            pltpu.VMEM((2, 128, 128), f32),
+            pltpu.VMEM((16, 128), jnp.int32),
+            pltpu.VMEM((16, 128), jnp.int32),
         ],
         compiler_params=pltpu.CompilerParams(
             collective_id=0, has_side_effects=True, vmem_limit_bytes=62 * 2**20
         ),
         cost_estimate=pl.CostEstimate(flops=2**35, bytes_accessed=50 * 2**20, transcendentals=0),
         name="whole",
-    )(own, pay, qry, passages, wq, wo, wu, wd, g1, g2)
+    )(p_own, p_row, o_own, o_clu, qry, passages, wq, wo, wu, wd, g1, g2)
 
 
 def on_device(
@@ -545,12 +563,9 @@
     gain_one,
     gain_two,
 ):
-    blank = jnp.full((Q_DEV, 60), -1, jnp.int32)
-    own = jnp.concatenate([pair_owner[:, :, 0], probe_owner, blank], 1)
-    pay = jnp.concatenate([pair_row, probe_cluster, blank * 0], 1)
     wq = jnp.transpose(w_qkv, (1, 0, 2))
     rows = whole(
-        own, pay, queries, passages, wq, w_out, w_up, w_down, gain_one[None, :], gain_two[None, :]
+        jnp.transpose(pair_owner, (0, 2, 1)), pair_row, probe_owner.T, probe_cluster.T, queries, passages, wq, w_out, w_up, w_down, gain_one[None, :], gain_two[None, :]
     )
     return jnp.transpose(rows.reshape(65, 16, D), (1, 0, 2))
 

time: 135 us -> 125 us (0.926)
  Pallas kernels: 128 us -> 121 us
  local copies, waits for them, and re-layouts: 4.92 us -> 3.25 us
  other arithmetic: 1.39 us -> 0 us
    pallas_call x1, Pallas kernels: 128 us -> 121 us  [whole(): pl.pallas_call(whole_kernel, out_shape=jax.ShapeDtypeStruct((N_TOK, D), b...]
    unnamed x3 -> x1, local copies, waits for them, and re-layouts: 4.76 us -> 3.25 us
    concatenate x1 -> x0, other arithmetic: 1.39 us -> none  [on_device(): own = jnp.concatenate([pair_owner[:, :, 0], probe_owner, blank], 1)]
where the time goes in v4:
time: 125 us; the launch traced here: 124 us
  Pallas kernels  121 us (97%)
  local copies, waits for them, and re-layouts  3.25 us (3%)
    pallas_call x1, Pallas kernels, whole(): pl.pallas_call(whole_kernel, out_shape=jax.ShapeDtypeStruct((N_TOK, D), b...  121 us
    unnamed x1, local copies, waits for them, and re-layouts  3.25 us

profile of v4, /device:TPU:1, one launch (start us, length us, event | category | flops | bytes accessed | tf_op | source)
XLA Modules:
  0.0 123.8 jit_solution(10767096664723220405)
XLA Ops:
  0.0 120.6 %whole.1 = bf16[1040,1024]{1,0:T(8,128)(2,1)} custom-call(s32[16,1,64]{2,1,0:T(1,128)} %bitcast.11, s32[16,64]{1,0:T(8,128)} %p_row.1, s32[4,16]{1,0:T(4,128)} %bitcast.14, s32[4,16]{1,0:T(4,128)} %bitcast.15, bf16[16,1024]{1,0:T(8,128)(2,1)} %qry.1, bf16[2048,1024]{1,0:T(8,128)(2,1)} %psg_in.1, bf16[3,1024,512]{2,1,0:T(8,128)(2,1)} %bitcast.10, ...), custom_call_target="tpu_custom_call" | custom-call | flops 34359738368 | bytes 52428800 | tf_op jit(solution)/shard_map/whole/pallas_call | solution.py:503
  120.6 3.2 %copy.14 = bf16[16,65,1024]{2,0,1:T(8,128)(2,1)} copy(bf16[16,65,1024]{2,0,1:T(8,128)(2,1)} %bitcast.9) | data formatting | bytes 4259840
